TPU v7x, 32 devices: a whole 2x2x4 slice. The times are simulated.
32 devices in a mesh: patch: 8 (over y, x, core), vgroup: 4 (over z).
Axes of the slice: x: 2, y: 2, z: 4, core: 2. Of those that a mesh axis runs over, the one named last changes fastest.
Arguments:
- exposures: bfloat16 [4, 256, 62, 2048], P('vgroup', 'patch'), may hold values from -6 to 6
- target_patch: int32 [4, 256, 1], P('vgroup'), may hold values from 0 to 7; in each aligned block of 32 rows (0 to 31, 32 to 63, ..., all dimensions but the last counted through in order) at most 8 rows name the same one
- row_offset: int32 [4, 256], P('vgroup'), may hold values from 0 to 224
- basis_index: int32 [4, 256, 3], P('vgroup'), may hold values from 0 to 34
- basis_coef: float32 [4, 256, 3], P('vgroup'), may hold values from 0.3 to 1.5
- inv_variance: float32 [4, 256], P('vgroup'), may hold values from 0.25 to 4
- psf_basis: float32 [35, 2, 31], replicated, may hold values from -1 to 1
Outputs:
- coadd: float32 [2048, 2048], P(('patch', 'vgroup'))
- weight_map: float32 [2048], P(('patch', 'vgroup'))
Inputs may be any that keep to these rules, and one draw needn't show every extreme that they name: `target_patch`: among the 32 blocks of one device (aligned blocks along the second dimension), at most 8 name the same patch, a bound that some block reaches of them.
All inputs are finite; a program needn't handle non-finite values.
Results may differ from a plain program's by a relative error of at most 0.003.
Values may be sent and summed in bfloat16 or wider, within the bound.
A program may use at most 128 MiB of HBM per device.

v0:
```python
import jax
import jax.numpy as jnp
from jax import lax
from jax.sharding import PartitionSpec as P

PR = 256


def psf_match(blocks, kernel_taps, coefficient):
    halo_rows = (kernel_taps.shape[-1] - 1) // 2
    columns = blocks.shape[-1]
    out_rows = blocks.shape[-2] - 2 * halo_rows
    pixels = blocks.astype(jnp.float32)
    padded = jnp.pad(pixels, [(0, 0)] * (pixels.ndim - 1) + [(halo_rows, halo_rows)])
    summed = jnp.zeros(pixels.shape[:-2] + (out_rows, columns), jnp.float32)
    for term_id in range(kernel_taps.shape[-3]):
        across = jnp.zeros_like(pixels)
        for tap_id in range(kernel_taps.shape[-1]):
            across = (
                across
                + kernel_taps[..., term_id, 1, tap_id, None, None]
                * padded[..., :, tap_id : tap_id + columns]
            )
        downward = jnp.zeros_like(summed)
        for tap_id in range(kernel_taps.shape[-1]):
            downward = (
                downward
                + kernel_taps[..., term_id, 0, tap_id, None, None]
                * across[..., tap_id : tap_id + out_rows, :]
            )
        summed = summed + coefficient[..., term_id, None, None] * downward
    return summed.astype(jnp.bfloat16)


def match_all(blocks, kernel_taps, coefficient):
    count = blocks.shape[0]
    groups = 8
    shaped = (
        blocks.reshape((groups, count // groups) + blocks.shape[1:]),
        kernel_taps.reshape((groups, count // groups) + kernel_taps.shape[1:]),
        coefficient.reshape((groups, count // groups) + coefficient.shape[1:]),
    )
    matched = lax.map(lambda members: psf_match(*members), shaped)
    return matched.reshape((count,) + matched.shape[2:])


def local(exposures, target_patch, row_offset, basis_index, basis_coef, inv_variance, psf_basis):
    n_patch = lax.axis_size("patch")
    own_patch = lax.axis_index("patch")
    blocks = exposures[0]
    per_device = blocks.shape[0]
    capacity = 2 * per_device // n_patch
    out_rows = blocks.shape[1] - (psf_basis.shape[-1] - 1)
    n_basis = psf_basis.shape[0]
    n_terms = basis_index.shape[-1]
    targets = target_patch[0, :, 0].reshape(n_patch, per_device)
    positions = jnp.arange(per_device, dtype=jnp.int32)
    same_patch = targets[:, :, None] == targets[:, None, :]
    earlier = positions[None, :, None] > positions[None, None, :]
    slot_rank = jnp.sum(jnp.logical_and(same_patch, earlier), axis=2)
    peer_ids = jnp.arange(n_patch, dtype=jnp.int32)
    slot_ids = jnp.arange(capacity, dtype=jnp.int32)
    one_hot = (basis_index[0][..., None] == jnp.arange(n_basis, dtype=jnp.int32)).astype(
        jnp.float32
    )
    taps_all = jnp.einsum(
        "btn,nk->btk", one_hot, psf_basis.reshape(n_basis, -1), precision=lax.Precision.HIGHEST
    )
    taps_all = taps_all.reshape(n_patch, per_device, -1)
    coef_all = basis_coef[0].reshape(n_patch, per_device, n_terms)
    own_target = lax.dynamic_slice_in_dim(targets, own_patch, 1, 0)[0]
    own_rank = lax.dynamic_slice_in_dim(slot_rank, own_patch, 1, 0)[0]
    source_pick = jnp.logical_and(
        own_target[None, None, :] == peer_ids[:, None, None],
        own_rank[None, None, :] == slot_ids[None, :, None],
    )
    source_index = jnp.sum(source_pick * positions[None, None, :], axis=2)
    present = jnp.any(source_pick, axis=2).astype(jnp.bfloat16)[:, :, None, None]
    taking = jnp.logical_and(
        targets[:, None, :] == own_patch, slot_rank[:, None, :] == slot_ids[None, :, None]
    )
    taking_float = taking.astype(jnp.float32)
    offsets_in = jnp.sum(taking * row_offset[0].reshape(n_patch, 1, per_device), axis=2)
    weights_in = jnp.einsum(
        "qcb,qb->qc",
        taking_float,
        inv_variance[0].reshape(n_patch, per_device),
        precision=lax.Precision.HIGHEST,
    )
    own_taps = lax.dynamic_slice_in_dim(taps_all, own_patch, 1, 0)[0]
    own_coef = lax.dynamic_slice_in_dim(coef_all, own_patch, 1, 0)[0]
    matched_own = match_all(blocks, own_taps.reshape(per_device, n_terms, 2, -1), own_coef)
    outgoing = matched_own[source_index] * present
    arrived = lax.all_to_all(outgoing, "patch", split_axis=0, concat_axis=0, tiled=True)
    matched = arrived.reshape((n_patch * capacity,) + arrived.shape[2:])
    slot_count = n_patch * capacity
    row_index = (
        offsets_in.reshape(slot_count)[:, None] + jnp.arange(out_rows, dtype=jnp.int32)[None, :]
    )
    placement = (row_index[None, :, :] == jnp.arange(PR, dtype=jnp.int32)[:, None, None]).astype(
        jnp.float32
    )
    placement = placement * weights_in.reshape(slot_count)[None, :, None]
    numerator = jnp.einsum(
        "rsi,siw->rw", placement, matched.astype(jnp.float32), precision=lax.Precision.HIGHEST
    )
    weight_sum = jnp.sum(placement, axis=(1, 2))
    numer_share, weight_share = (
        lax.psum_scatter(numerator, "vgroup", scatter_dimension=0, tiled=True),
        lax.psum_scatter(weight_sum, "vgroup", scatter_dimension=0, tiled=True),
    )
    coadd = numer_share / (1.0 + weight_share[:, None])
    return (coadd, weight_share)


def solution(mesh):
    in_specs = (
        P("vgroup", "patch", None, None),
        P("vgroup", None, None),
        P("vgroup", None),
        P("vgroup", None, None),
        P("vgroup", None, None),
        P("vgroup", None),
        P(),
    )
    out_specs = (P(("patch", "vgroup"), None), P(("patch", "vgroup")))
    return jax.shard_map(local, mesh=mesh, in_specs=in_specs, out_specs=out_specs, check_vma=False)
```

profile of v0, /device:TPU:0, one launch (start us, length us, event | category | flops | bytes accessed | tf_op | source)
XLA Modules:
  0.0 1247.0 jit_solution(16000005806153972536)
XLA Ops:
  15.1 11.0 copy.38
  26.2 1029.8 %while.12 = (s32[]{:T(128)}, bf16[8,4,32,2048]{3,2,1,0:T(8,128)(2,1)}, f32[8,4,3]{2,1,0:T(4,128)S(1)}, f32[8,4,3,2,31]{4,3,2,1,0:T(2,128)S(1)}, bf16[8,4,62,2048]{3,2,1,0:T(8,128)(2,1)}, /*index=5*/s32[]{:T(128)}) while((s32[]{:T(128)}, bf16[8,4,32,2048]{3,2,1,0:T(8,128)(2,1)}, f32[8,4,3]{2,1,0:T(4,128)S(1)}, ...), condition=%wide.region_3.0_spmd, body=%wide.region_2.0_spmd.sunk | while | flops 142999552 | bytes 121426632 | solution.py:43
  26.4 2.8 bitcast_convert_fusion.2
  29.5 42.1 %multiply_add_fusion.6 = f32[4,62,2048]{2,1,0:T(8,128)S(1)} fusion(f32[4,62,2048]{2,1,0:T(8,128)} %bitcast_convert_fusion.2, f32[4]{0:T(128)S(1)} %get-tuple-element.516, f32[4]{0:T(128)S(1)} %get-tuple-element.517, f32[4]{0:T(128)S(1)} %get-tuple-element.518, f32[4]{0:T(128)S(1)} %get-tuple-element.519, f32[4]{0:T(128)S(1)} %get-tuple-element.520, ...), kind=kLoop, calls=%fused_computation.1.clone.1 | loop fusion | flops 30982144 | bytes 4063728 | tf_op jit(solution)/shard_map/while/body/eval_jaxpr/add | solution.py:20
  71.8 17.5 %multiply_add_fusion.7 = f32[4,62,2048]{2,1,0:T(8,128)} fusion(f32[4,62,2048]{2,1,0:T(8,128)S(1)} %copy-done, f32[4]{0:T(128)S(1)} %get-tuple-element.579, f32[4]{0:T(128)S(1)} %get-tuple-element.580, f32[4]{0:T(128)S(1)} %get-tuple-element.581, f32[4]{0:T(128)S(1)} %get-tuple-element.582, f32[4]{0:T(128)S(1)} %get-tuple-element.583, ...), kind=kLoop, calls=%fused_computation.2.clone.1 | loop fusion | flops 30982144 | bytes 4063728 | tf_op jit(solution)/shard_map/while/body/eval_jaxpr/add | solution.py:20
  89.3 17.5 %multiply_add_fusion.8 = f32[4,62,2048]{2,1,0:T(8,128)} fusion(f32[4,62,2048]{2,1,0:T(8,128)S(1)} %copy-done, f32[4]{0:T(128)S(1)} %get-tuple-element.642, f32[4]{0:T(128)S(1)} %get-tuple-element.643, f32[4]{0:T(128)S(1)} %get-tuple-element.644, f32[4]{0:T(128)S(1)} %get-tuple-element.645, f32[4]{0:T(128)S(1)} %get-tuple-element.646, ...), kind=kLoop, calls=%fused_computation.3.clone.1 | loop fusion | flops 30982144 | bytes 4063728 | tf_op jit(solution)/shard_map/while/body/eval_jaxpr/add | solution.py:20
  106.8 47.2 %bitcast_dynamic-update-slice_fusion.2 = bf16[8,4,32,2048]{3,2,1,0:T(8,128)(2,1)} fusion(bf16[8,4,32,2048]{3,2,1,0:T(8,128)(2,1)} %get-tuple-element.712, s32[]{:T(128)S(6)} %copy.63, f32[4,62,2048]{2,1,0:T(8,128)S(1)} %multiply_add_fusion.6, f32[4]{0:T(128)S(1)} %get-tuple-element.547, f32[4]{0:T(128)S(1)} %get-tuple-element.548, ...), kind=kLoop, calls=%fused_computation.223.clone.1 | loop fusion | flops 49545216 | bytes 98043392 | tf_op jit(solution)/shard_map/while/body/jit(dynamic_update_index_in_dim)/dynamic_update_slice | solution.py:43
  154.0 2.8 bitcast_convert_fusion.2
  157.1 42.1 %multiply_add_fusion.6 = f32[4,62,2048]{2,1,0:T(8,128)S(1)} fusion(f32[4,62,2048]{2,1,0:T(8,128)} %bitcast_convert_fusion.2, f32[4]{0:T(128)S(1)} %get-tuple-element.516, f32[4]{0:T(128)S(1)} %get-tuple-element.517, f32[4]{0:T(128)S(1)} %get-tuple-element.518, f32[4]{0:T(128)S(1)} %get-tuple-element.519, f32[4]{0:T(128)S(1)} %get-tuple-element.520, ...), kind=kLoop, calls=%fused_computation.1.clone.1 | loop fusion | flops 30982144 | bytes 4063728 | tf_op jit(solution)/shard_map/while/body/eval_jaxpr/add | solution.py:20
  199.4 17.5 %multiply_add_fusion.7 = f32[4,62,2048]{2,1,0:T(8,128)} fusion(f32[4,62,2048]{2,1,0:T(8,128)S(1)} %copy-done, f32[4]{0:T(128)S(1)} %get-tuple-element.579, f32[4]{0:T(128)S(1)} %get-tuple-element.580, f32[4]{0:T(128)S(1)} %get-tuple-element.581, f32[4]{0:T(128)S(1)} %get-tuple-element.582, f32[4]{0:T(128)S(1)} %get-tuple-element.583, ...), kind=kLoop, calls=%fused_computation.2.clone.1 | loop fusion | flops 30982144 | bytes 4063728 | tf_op jit(solution)/shard_map/while/body/eval_jaxpr/add | solution.py:20
  216.9 17.5 %multiply_add_fusion.8 = f32[4,62,2048]{2,1,0:T(8,128)} fusion(f32[4,62,2048]{2,1,0:T(8,128)S(1)} %copy-done, f32[4]{0:T(128)S(1)} %get-tuple-element.642, f32[4]{0:T(128)S(1)} %get-tuple-element.643, f32[4]{0:T(128)S(1)} %get-tuple-element.644, f32[4]{0:T(128)S(1)} %get-tuple-element.645, f32[4]{0:T(128)S(1)} %get-tuple-element.646, ...), kind=kLoop, calls=%fused_computation.3.clone.1 | loop fusion | flops 30982144 | bytes 4063728 | tf_op jit(solution)/shard_map/while/body/eval_jaxpr/add | solution.py:20
  234.5 47.2 %bitcast_dynamic-update-slice_fusion.2 = bf16[8,4,32,2048]{3,2,1,0:T(8,128)(2,1)} fusion(bf16[8,4,32,2048]{3,2,1,0:T(8,128)(2,1)} %get-tuple-element.712, s32[]{:T(128)S(6)} %copy.63, f32[4,62,2048]{2,1,0:T(8,128)S(1)} %multiply_add_fusion.6, f32[4]{0:T(128)S(1)} %get-tuple-element.547, f32[4]{0:T(128)S(1)} %get-tuple-element.548, ...), kind=kLoop, calls=%fused_computation.223.clone.1 | loop fusion | flops 49545216 | bytes 98043392 | tf_op jit(solution)/shard_map/while/body/jit(dynamic_update_index_in_dim)/dynamic_update_slice | solution.py:43
  281.6 2.8 bitcast_convert_fusion.2
  284.7 42.1 %multiply_add_fusion.6 = f32[4,62,2048]{2,1,0:T(8,128)S(1)} fusion(f32[4,62,2048]{2,1,0:T(8,128)} %bitcast_convert_fusion.2, f32[4]{0:T(128)S(1)} %get-tuple-element.516, f32[4]{0:T(128)S(1)} %get-tuple-element.517, f32[4]{0:T(128)S(1)} %get-tuple-element.518, f32[4]{0:T(128)S(1)} %get-tuple-element.519, f32[4]{0:T(128)S(1)} %get-tuple-element.520, ...), kind=kLoop, calls=%fused_computation.1.clone.1 | loop fusion | flops 30982144 | bytes 4063728 | tf_op jit(solution)/shard_map/while/body/eval_jaxpr/add | solution.py:20
  327.1 17.5 %multiply_add_fusion.7 = f32[4,62,2048]{2,1,0:T(8,128)} fusion(f32[4,62,2048]{2,1,0:T(8,128)S(1)} %copy-done, f32[4]{0:T(128)S(1)} %get-tuple-element.579, f32[4]{0:T(128)S(1)} %get-tuple-element.580, f32[4]{0:T(128)S(1)} %get-tuple-element.581, f32[4]{0:T(128)S(1)} %get-tuple-element.582, f32[4]{0:T(128)S(1)} %get-tuple-element.583, ...), kind=kLoop, calls=%fused_computation.2.clone.1 | loop fusion | flops 30982144 | bytes 4063728 | tf_op jit(solution)/shard_map/while/body/eval_jaxpr/add | solution.py:20
  344.6 17.5 %multiply_add_fusion.8 = f32[4,62,2048]{2,1,0:T(8,128)} fusion(f32[4,62,2048]{2,1,0:T(8,128)S(1)} %copy-done, f32[4]{0:T(128)S(1)} %get-tuple-element.642, f32[4]{0:T(128)S(1)} %get-tuple-element.643, f32[4]{0:T(128)S(1)} %get-tuple-element.644, f32[4]{0:T(128)S(1)} %get-tuple-element.645, f32[4]{0:T(128)S(1)} %get-tuple-element.646, ...), kind=kLoop, calls=%fused_computation.3.clone.1 | loop fusion | flops 30982144 | bytes 4063728 | tf_op jit(solution)/shard_map/while/body/eval_jaxpr/add | solution.py:20
  362.1 47.2 %bitcast_dynamic-update-slice_fusion.2 = bf16[8,4,32,2048]{3,2,1,0:T(8,128)(2,1)} fusion(bf16[8,4,32,2048]{3,2,1,0:T(8,128)(2,1)} %get-tuple-element.712, s32[]{:T(128)S(6)} %copy.63, f32[4,62,2048]{2,1,0:T(8,128)S(1)} %multiply_add_fusion.6, f32[4]{0:T(128)S(1)} %get-tuple-element.547, f32[4]{0:T(128)S(1)} %get-tuple-element.548, ...), kind=kLoop, calls=%fused_computation.223.clone.1 | loop fusion | flops 49545216 | bytes 98043392 | tf_op jit(solution)/shard_map/while/body/jit(dynamic_update_index_in_dim)/dynamic_update_slice | solution.py:43
  409.3 2.8 bitcast_convert_fusion.2
  412.3 42.1 %multiply_add_fusion.6 = f32[4,62,2048]{2,1,0:T(8,128)S(1)} fusion(f32[4,62,2048]{2,1,0:T(8,128)} %bitcast_convert_fusion.2, f32[4]{0:T(128)S(1)} %get-tuple-element.516, f32[4]{0:T(128)S(1)} %get-tuple-element.517, f32[4]{0:T(128)S(1)} %get-tuple-element.518, f32[4]{0:T(128)S(1)} %get-tuple-element.519, f32[4]{0:T(128)S(1)} %get-tuple-element.520, ...), kind=kLoop, calls=%fused_computation.1.clone.1 | loop fusion | flops 30982144 | bytes 4063728 | tf_op jit(solution)/shard_map/while/body/eval_jaxpr/add | solution.py:20
  454.7 17.5 %multiply_add_fusion.7 = f32[4,62,2048]{2,1,0:T(8,128)} fusion(f32[4,62,2048]{2,1,0:T(8,128)S(1)} %copy-done, f32[4]{0:T(128)S(1)} %get-tuple-element.579, f32[4]{0:T(128)S(1)} %get-tuple-element.580, f32[4]{0:T(128)S(1)} %get-tuple-element.581, f32[4]{0:T(128)S(1)} %get-tuple-element.582, f32[4]{0:T(128)S(1)} %get-tuple-element.583, ...), kind=kLoop, calls=%fused_computation.2.clone.1 | loop fusion | flops 30982144 | bytes 4063728 | tf_op jit(solution)/shard_map/while/body/eval_jaxpr/add | solution.py:20
  472.2 17.5 %multiply_add_fusion.8 = f32[4,62,2048]{2,1,0:T(8,128)} fusion(f32[4,62,2048]{2,1,0:T(8,128)S(1)} %copy-done, f32[4]{0:T(128)S(1)} %get-tuple-element.642, f32[4]{0:T(128)S(1)} %get-tuple-element.643, f32[4]{0:T(128)S(1)} %get-tuple-element.644, f32[4]{0:T(128)S(1)} %get-tuple-element.645, f32[4]{0:T(128)S(1)} %get-tuple-element.646, ...), kind=kLoop, calls=%fused_computation.3.clone.1 | loop fusion | flops 30982144 | bytes 4063728 | tf_op jit(solution)/shard_map/while/body/eval_jaxpr/add | solution.py:20
  489.7 47.2 %bitcast_dynamic-update-slice_fusion.2 = bf16[8,4,32,2048]{3,2,1,0:T(8,128)(2,1)} fusion(bf16[8,4,32,2048]{3,2,1,0:T(8,128)(2,1)} %get-tuple-element.712, s32[]{:T(128)S(6)} %copy.63, f32[4,62,2048]{2,1,0:T(8,128)S(1)} %multiply_add_fusion.6, f32[4]{0:T(128)S(1)} %get-tuple-element.547, f32[4]{0:T(128)S(1)} %get-tuple-element.548, ...), kind=kLoop, calls=%fused_computation.223.clone.1 | loop fusion | flops 49545216 | bytes 98043392 | tf_op jit(solution)/shard_map/while/body/jit(dynamic_update_index_in_dim)/dynamic_update_slice | solution.py:43
  540.0 42.1 %multiply_add_fusion.6 = f32[4,62,2048]{2,1,0:T(8,128)S(1)} fusion(f32[4,62,2048]{2,1,0:T(8,128)} %bitcast_convert_fusion.2, f32[4]{0:T(128)S(1)} %get-tuple-element.516, f32[4]{0:T(128)S(1)} %get-tuple-element.517, f32[4]{0:T(128)S(1)} %get-tuple-element.518, f32[4]{0:T(128)S(1)} %get-tuple-element.519, f32[4]{0:T(128)S(1)} %get-tuple-element.520, ...), kind=kLoop, calls=%fused_computation.1.clone.1 | loop fusion | flops 30982144 | bytes 4063728 | tf_op jit(solution)/shard_map/while/body/eval_jaxpr/add | solution.py:20
  582.3 17.5 %multiply_add_fusion.7 = f32[4,62,2048]{2,1,0:T(8,128)} fusion(f32[4,62,2048]{2,1,0:T(8,128)S(1)} %copy-done, f32[4]{0:T(128)S(1)} %get-tuple-element.579, f32[4]{0:T(128)S(1)} %get-tuple-element.580, f32[4]{0:T(128)S(1)} %get-tuple-element.581, f32[4]{0:T(128)S(1)} %get-tuple-element.582, f32[4]{0:T(128)S(1)} %get-tuple-element.583, ...), kind=kLoop, calls=%fused_computation.2.clone.1 | loop fusion | flops 30982144 | bytes 4063728 | tf_op jit(solution)/shard_map/while/body/eval_jaxpr/add | solution.py:20
  599.8 17.5 %multiply_add_fusion.8 = f32[4,62,2048]{2,1,0:T(8,128)} fusion(f32[4,62,2048]{2,1,0:T(8,128)S(1)} %copy-done, f32[4]{0:T(128)S(1)} %get-tuple-element.642, f32[4]{0:T(128)S(1)} %get-tuple-element.643, f32[4]{0:T(128)S(1)} %get-tuple-element.644, f32[4]{0:T(128)S(1)} %get-tuple-element.645, f32[4]{0:T(128)S(1)} %get-tuple-element.646, ...), kind=kLoop, calls=%fused_computation.3.clone.1 | loop fusion | flops 30982144 | bytes 4063728 | tf_op jit(solution)/shard_map/while/body/eval_jaxpr/add | solution.py:20
  617.4 47.2 %bitcast_dynamic-update-slice_fusion.2 = bf16[8,4,32,2048]{3,2,1,0:T(8,128)(2,1)} fusion(bf16[8,4,32,2048]{3,2,1,0:T(8,128)(2,1)} %get-tuple-element.712, s32[]{:T(128)S(6)} %copy.63, f32[4,62,2048]{2,1,0:T(8,128)S(1)} %multiply_add_fusion.6, f32[4]{0:T(128)S(1)} %get-tuple-element.547, f32[4]{0:T(128)S(1)} %get-tuple-element.548, ...), kind=kLoop, calls=%fused_computation.223.clone.1 | loop fusion | flops 49545216 | bytes 98043392 | tf_op jit(solution)/shard_map/while/body/jit(dynamic_update_index_in_dim)/dynamic_update_slice | solution.py:43
  664.6 2.8 bitcast_convert_fusion.2
  667.6 42.1 %multiply_add_fusion.6 = f32[4,62,2048]{2,1,0:T(8,128)S(1)} fusion(f32[4,62,2048]{2,1,0:T(8,128)} %bitcast_convert_fusion.2, f32[4]{0:T(128)S(1)} %get-tuple-element.516, f32[4]{0:T(128)S(1)} %get-tuple-element.517, f32[4]{0:T(128)S(1)} %get-tuple-element.518, f32[4]{0:T(128)S(1)} %get-tuple-element.519, f32[4]{0:T(128)S(1)} %get-tuple-element.520, ...), kind=kLoop, calls=%fused_computation.1.clone.1 | loop fusion | flops 30982144 | bytes 4063728 | tf_op jit(solution)/shard_map/while/body/eval_jaxpr/add | solution.py:20
  710.0 17.5 %multiply_add_fusion.7 = f32[4,62,2048]{2,1,0:T(8,128)} fusion(f32[4,62,2048]{2,1,0:T(8,128)S(1)} %copy-done, f32[4]{0:T(128)S(1)} %get-tuple-element.579, f32[4]{0:T(128)S(1)} %get-tuple-element.580, f32[4]{0:T(128)S(1)} %get-tuple-element.581, f32[4]{0:T(128)S(1)} %get-tuple-element.582, f32[4]{0:T(128)S(1)} %get-tuple-element.583, ...), kind=kLoop, calls=%fused_computation.2.clone.1 | loop fusion | flops 30982144 | bytes 4063728 | tf_op jit(solution)/shard_map/while/body/eval_jaxpr/add | solution.py:20
  727.5 17.5 %multiply_add_fusion.8 = f32[4,62,2048]{2,1,0:T(8,128)} fusion(f32[4,62,2048]{2,1,0:T(8,128)S(1)} %copy-done, f32[4]{0:T(128)S(1)} %get-tuple-element.642, f32[4]{0:T(128)S(1)} %get-tuple-element.643, f32[4]{0:T(128)S(1)} %get-tuple-element.644, f32[4]{0:T(128)S(1)} %get-tuple-element.645, f32[4]{0:T(128)S(1)} %get-tuple-element.646, ...), kind=kLoop, calls=%fused_computation.3.clone.1 | loop fusion | flops 30982144 | bytes 4063728 | tf_op jit(solution)/shard_map/while/body/eval_jaxpr/add | solution.py:20
  745.0 47.2 %bitcast_dynamic-update-slice_fusion.2 = bf16[8,4,32,2048]{3,2,1,0:T(8,128)(2,1)} fusion(bf16[8,4,32,2048]{3,2,1,0:T(8,128)(2,1)} %get-tuple-element.712, s32[]{:T(128)S(6)} %copy.63, f32[4,62,2048]{2,1,0:T(8,128)S(1)} %multiply_add_fusion.6, f32[4]{0:T(128)S(1)} %get-tuple-element.547, f32[4]{0:T(128)S(1)} %get-tuple-element.548, ...), kind=kLoop, calls=%fused_computation.223.clone.1 | loop fusion | flops 49545216 | bytes 98043392 | tf_op jit(solution)/shard_map/while/body/jit(dynamic_update_index_in_dim)/dynamic_update_slice | solution.py:43
  795.2 42.1 %multiply_add_fusion.6 = f32[4,62,2048]{2,1,0:T(8,128)S(1)} fusion(f32[4,62,2048]{2,1,0:T(8,128)} %bitcast_convert_fusion.2, f32[4]{0:T(128)S(1)} %get-tuple-element.516, f32[4]{0:T(128)S(1)} %get-tuple-element.517, f32[4]{0:T(128)S(1)} %get-tuple-element.518, f32[4]{0:T(128)S(1)} %get-tuple-element.519, f32[4]{0:T(128)S(1)} %get-tuple-element.520, ...), kind=kLoop, calls=%fused_computation.1.clone.1 | loop fusion | flops 30982144 | bytes 4063728 | tf_op jit(solution)/shard_map/while/body/eval_jaxpr/add | solution.py:20
  837.6 17.5 %multiply_add_fusion.7 = f32[4,62,2048]{2,1,0:T(8,128)} fusion(f32[4,62,2048]{2,1,0:T(8,128)S(1)} %copy-done, f32[4]{0:T(128)S(1)} %get-tuple-element.579, f32[4]{0:T(128)S(1)} %get-tuple-element.580, f32[4]{0:T(128)S(1)} %get-tuple-element.581, f32[4]{0:T(128)S(1)} %get-tuple-element.582, f32[4]{0:T(128)S(1)} %get-tuple-element.583, ...), kind=kLoop, calls=%fused_computation.2.clone.1 | loop fusion | flops 30982144 | bytes 4063728 | tf_op jit(solution)/shard_map/while/body/eval_jaxpr/add | solution.py:20
  855.1 17.5 %multiply_add_fusion.8 = f32[4,62,2048]{2,1,0:T(8,128)} fusion(f32[4,62,2048]{2,1,0:T(8,128)S(1)} %copy-done, f32[4]{0:T(128)S(1)} %get-tuple-element.642, f32[4]{0:T(128)S(1)} %get-tuple-element.643, f32[4]{0:T(128)S(1)} %get-tuple-element.644, f32[4]{0:T(128)S(1)} %get-tuple-element.645, f32[4]{0:T(128)S(1)} %get-tuple-element.646, ...), kind=kLoop, calls=%fused_computation.3.clone.1 | loop fusion | flops 30982144 | bytes 4063728 | tf_op jit(solution)/shard_map/while/body/eval_jaxpr/add | solution.py:20
  872.6 47.2 %bitcast_dynamic-update-slice_fusion.2 = bf16[8,4,32,2048]{3,2,1,0:T(8,128)(2,1)} fusion(bf16[8,4,32,2048]{3,2,1,0:T(8,128)(2,1)} %get-tuple-element.712, s32[]{:T(128)S(6)} %copy.63, f32[4,62,2048]{2,1,0:T(8,128)S(1)} %multiply_add_fusion.6, f32[4]{0:T(128)S(1)} %get-tuple-element.547, f32[4]{0:T(128)S(1)} %get-tuple-element.548, ...), kind=kLoop, calls=%fused_computation.223.clone.1 | loop fusion | flops 49545216 | bytes 98043392 | tf_op jit(solution)/shard_map/while/body/jit(dynamic_update_index_in_dim)/dynamic_update_slice | solution.py:43
  919.8 2.8 bitcast_convert_fusion.2
  922.9 42.1 %multiply_add_fusion.6 = f32[4,62,2048]{2,1,0:T(8,128)S(1)} fusion(f32[4,62,2048]{2,1,0:T(8,128)} %bitcast_convert_fusion.2, f32[4]{0:T(128)S(1)} %get-tuple-element.516, f32[4]{0:T(128)S(1)} %get-tuple-element.517, f32[4]{0:T(128)S(1)} %get-tuple-element.518, f32[4]{0:T(128)S(1)} %get-tuple-element.519, f32[4]{0:T(128)S(1)} %get-tuple-element.520, ...), kind=kLoop, calls=%fused_computation.1.clone.1 | loop fusion | flops 30982144 | bytes 4063728 | tf_op jit(solution)/shard_map/while/body/eval_jaxpr/add | solution.py:20
  965.2 17.5 %multiply_add_fusion.7 = f32[4,62,2048]{2,1,0:T(8,128)} fusion(f32[4,62,2048]{2,1,0:T(8,128)S(1)} %copy-done, f32[4]{0:T(128)S(1)} %get-tuple-element.579, f32[4]{0:T(128)S(1)} %get-tuple-element.580, f32[4]{0:T(128)S(1)} %get-tuple-element.581, f32[4]{0:T(128)S(1)} %get-tuple-element.582, f32[4]{0:T(128)S(1)} %get-tuple-element.583, ...), kind=kLoop, calls=%fused_computation.2.clone.1 | loop fusion | flops 30982144 | bytes 4063728 | tf_op jit(solution)/shard_map/while/body/eval_jaxpr/add | solution.py:20
  982.7 17.5 %multiply_add_fusion.8 = f32[4,62,2048]{2,1,0:T(8,128)} fusion(f32[4,62,2048]{2,1,0:T(8,128)S(1)} %copy-done, f32[4]{0:T(128)S(1)} %get-tuple-element.642, f32[4]{0:T(128)S(1)} %get-tuple-element.643, f32[4]{0:T(128)S(1)} %get-tuple-element.644, f32[4]{0:T(128)S(1)} %get-tuple-element.645, f32[4]{0:T(128)S(1)} %get-tuple-element.646, ...), kind=kLoop, calls=%fused_computation.3.clone.1 | loop fusion | flops 30982144 | bytes 4063728 | tf_op jit(solution)/shard_map/while/body/eval_jaxpr/add | solution.py:20
  1000.2 47.2 %bitcast_dynamic-update-slice_fusion.2 = bf16[8,4,32,2048]{3,2,1,0:T(8,128)(2,1)} fusion(bf16[8,4,32,2048]{3,2,1,0:T(8,128)(2,1)} %get-tuple-element.712, s32[]{:T(128)S(6)} %copy.63, f32[4,62,2048]{2,1,0:T(8,128)S(1)} %multiply_add_fusion.6, f32[4]{0:T(128)S(1)} %get-tuple-element.547, f32[4]{0:T(128)S(1)} %get-tuple-element.548, ...), kind=kLoop, calls=%fused_computation.223.clone.1 | loop fusion | flops 49545216 | bytes 98043392 | tf_op jit(solution)/shard_map/while/body/jit(dynamic_update_index_in_dim)/dynamic_update_slice | solution.py:43
  1056.1 7.6 gather_fusion
  1063.7 7.2 broadcast_multiply_fusion
  1070.9 12.1 copy.41
  1083.0 5.3 all-to-all-start
  1090.9 91.9 %all-to-all-done = bf16[8,8,32,2048]{3,1,2,0:T(8,128)(2,1)} async-done(((bf16[8,8,32,2048]{3,1,2,0:T(8,128)(2,1)}), bf16[8,8,32,2048]{3,1,2,0:T(8,128)(2,1)}, u32[]{:S(2)}, u32[]{:S(2)}) %all-to-all-start) | async-done | bytes 8388640 | tf_op jit(solution)/shard_map/all_to_all | solution.py:94
  1182.8 10.9 fusion.100
  1196.1 13.0 %all-reduce.1 = f32[256]{0:T(256)S(1)} all-reduce(f32[256]{0:T(256)S(1)} %select_reduce_fusion), channel_id=3, replica_groups=mesh['patch'=8,'vgroup'=4] {'vgroup'}, use_global_device_ids=true, to_apply=%region_8.9.clone | all-reduce | flops 256 | bytes 2048
  1209.7 28.3 %reduce-scatter.2.cloned.1.call-done = f32[64,2048]{1,0:T(8,128)} async-done(((f32[256,2048]{1,0:T(8,128)}), f32[64,2048]{1,0:T(8,128)}) %reduce-scatter.2.cloned.1.call-update) | async-done | bytes 524304 | tf_op jit(solution)/shard_map/reduce_scatter | solution.py:109
  (192 shorter events, 24.1 us)
Async XLA Ops:
  9.1 3.3 copy-start.1
  9.4 0.6 copy-start.3
  26.1 1029.8 %copy-start.5 = (s32[8,8]{1,0:T(8,128)S(1)}, s32[8,8]{1,0:T(8,128)}, u32[]{:S(2)}) copy-start(s32[8,8]{1,0:T(8,128)} %fusion.110) | copy-start | bytes 772
  26.1 1029.9 %copy-start.6 = (pred[8,8]{1,0:T(8,128)(4,1)S(1)}, pred[8,8]{1,0:T(8,128)(4,1)}, u32[]{:S(2)}) copy-start(pred[8,8]{1,0:T(8,128)(4,1)} %and_reduce_fusion) | copy-start | bytes 196
  29.4 42.4 %copy-start = (f32[4,62,2048]{2,1,0:T(8,128)S(1)}, f32[4,62,2048]{2,1,0:T(8,128)}, u32[]{:S(2)}) copy-start(f32[4,62,2048]{2,1,0:T(8,128)} %bitcast_convert_fusion.2) | copy-start | bytes 6094852 | tf_op jit(solution)/shard_map/while
  157.1 42.4 %copy-start = (f32[4,62,2048]{2,1,0:T(8,128)S(1)}, f32[4,62,2048]{2,1,0:T(8,128)}, u32[]{:S(2)}) copy-start(f32[4,62,2048]{2,1,0:T(8,128)} %bitcast_convert_fusion.2) | copy-start | bytes 6094852 | tf_op jit(solution)/shard_map/while
  284.7 42.4 %copy-start = (f32[4,62,2048]{2,1,0:T(8,128)S(1)}, f32[4,62,2048]{2,1,0:T(8,128)}, u32[]{:S(2)}) copy-start(f32[4,62,2048]{2,1,0:T(8,128)} %bitcast_convert_fusion.2) | copy-start | bytes 6094852 | tf_op jit(solution)/shard_map/while
  412.3 42.4 %copy-start = (f32[4,62,2048]{2,1,0:T(8,128)S(1)}, f32[4,62,2048]{2,1,0:T(8,128)}, u32[]{:S(2)}) copy-start(f32[4,62,2048]{2,1,0:T(8,128)} %bitcast_convert_fusion.2) | copy-start | bytes 6094852 | tf_op jit(solution)/shard_map/while
  540.0 42.4 %copy-start = (f32[4,62,2048]{2,1,0:T(8,128)S(1)}, f32[4,62,2048]{2,1,0:T(8,128)}, u32[]{:S(2)}) copy-start(f32[4,62,2048]{2,1,0:T(8,128)} %bitcast_convert_fusion.2) | copy-start | bytes 6094852 | tf_op jit(solution)/shard_map/while
  667.6 42.4 %copy-start = (f32[4,62,2048]{2,1,0:T(8,128)S(1)}, f32[4,62,2048]{2,1,0:T(8,128)}, u32[]{:S(2)}) copy-start(f32[4,62,2048]{2,1,0:T(8,128)} %bitcast_convert_fusion.2) | copy-start | bytes 6094852 | tf_op jit(solution)/shard_map/while
  795.2 42.4 %copy-start = (f32[4,62,2048]{2,1,0:T(8,128)S(1)}, f32[4,62,2048]{2,1,0:T(8,128)}, u32[]{:S(2)}) copy-start(f32[4,62,2048]{2,1,0:T(8,128)} %bitcast_convert_fusion.2) | copy-start | bytes 6094852 | tf_op jit(solution)/shard_map/while
  922.9 42.4 %copy-start = (f32[4,62,2048]{2,1,0:T(8,128)S(1)}, f32[4,62,2048]{2,1,0:T(8,128)}, u32[]{:S(2)}) copy-start(f32[4,62,2048]{2,1,0:T(8,128)} %bitcast_convert_fusion.2) | copy-start | bytes 6094852 | tf_op jit(solution)/shard_map/while
  1083.0 5.9 copy-start.7
  1083.0 6.6 copy-start.2
  1083.0 6.6 copy-start.4
  1083.0 6.8 copy-start.8
  1083.0 99.8 %all-to-all-start = ((bf16[8,8,32,2048]{3,1,2,0:T(8,128)(2,1)}), bf16[8,8,32,2048]{3,1,2,0:T(8,128)(2,1)}, u32[]{:S(2)}, u32[]{:S(2)}) async-start(bf16[8,8,32,2048]{3,1,2,0:T(8,128)(2,1)} %copy.41), calls=%async_computation | async-start | bytes 16777216 | tf_op jit(solution)/shard_map/all_to_all | solution.py:94
  1088.3 149.7 %reduce-scatter.2.cloned.1.call-start = ((), (), s32[]{:S(2)}) async-start(), calls=%async_computation.2 | async-start | bytes 2621440 | tf_op jit(solution)/shard_map/reduce_scatter | solution.py:109
  1193.7 0.7 copy-start.9
Sparse Core Ops, SparseCore 0:
  1193.9 44.0 reduce-scatter.1
where the time goes:
time: 1250 us
  other arithmetic  1030 us (82%)
  waiting for transfers between devices  120 us (10%)
  local copies, waits for them, and re-layouts  40.1 us (3%)
  between operations  15 us (1%)
  blocking collectives  13 us (1%)
    add x24, other arithmetic, psf_match(): across + kernel_taps[..., term_id, 1, tap_id, None, None] * padded[..., :...  616 us
    dynamic_update_slice x8, other arithmetic, match_all(): matched = lax.map(lambda members: psf_match(*members), shaped)  377 us
    all_to_all x1, waiting for transfers between devices, local(): lax.all_to_all(outgoing, 'patch', split_axis=0, concat_axis=0, tiled=True)  91.9 us
    reduce_scatter x1, waiting for transfers between devices, local(): lax.psum_scatter(numerator, 'vgroup', scatter_dimension=0, tiled=True)  28.3 us
  transfers between devices with their start and end apart: 2, of which 2 were waited for; matrix products, arithmetic and copies ran while one was open for 0% of the time, Pallas kernels for 0%

commit v1 on v0

v1 whole, which is shorter than its diff:
```python
import functools

import jax
import jax.numpy as jnp
from jax import lax
from jax.experimental import pallas as pl
from jax.experimental.pallas import tpu as pltpu
from jax.sharding import PartitionSpec as P

PR = 256
LANES = 128
DENSE_LIMIT = 24 * 1024 * 1024
VMEM_LIMIT = 60 * 1024 * 1024


def split_bf16(values):
    high = values.astype(jnp.bfloat16)
    low = (values - high.astype(jnp.float32)).astype(jnp.bfloat16)
    return high, low


def build_tables(basis_ref, down_table, across_table, n_basis, taps):
    half = (taps - 1) // 2
    first = LANES // 2 - half

    def build(b, carry):
        line = basis_ref[b]
        down = pltpu.roll(
            jnp.broadcast_to(line[0:1, :], (32, LANES)), 0, 1, stride=1, stride_axis=0
        )
        down_table[b] = down
        reverse = jnp.broadcast_to(line[1:2, :], (2 * LANES, LANES))
        band = pltpu.roll(reverse, 0, 1, stride=1, stride_axis=0)
        tap = (
            lax.broadcasted_iota(jnp.int32, band.shape, 0)
            - lax.broadcasted_iota(jnp.int32, band.shape, 1)
            - first
        )
        band = jnp.where(jnp.logical_and(tap >= 0, tap < taps), band, 0.0)
        high, low = split_bf16(band)
        across_table[b, :, 0:LANES] = high
        across_table[b, :, LANES : 2 * LANES] = low
        return carry

    lax.fori_loop(0, n_basis, build, 0)


def match_block(b, index_ref, coef_ref, blocks_ref, pixels, windows, down_table, across_table, n_terms):
    in_rows, columns = blocks_ref.shape[1:]
    tiles = columns // LANES
    block = blocks_ref[b]
    pixels[0:in_rows, :] = block
    pixels[64 : 64 + in_rows, :] = block
    picks = [index_ref[b * n_terms + t] for t in range(n_terms)]
    rows = jnp.concatenate(
        [coef_ref[b * n_terms + t] * down_table[picks[t]] for t in range(n_terms)], axis=0
    )
    rows_high = rows.astype(jnp.bfloat16).astype(jnp.float32)
    lane = lax.broadcasted_iota(jnp.int32, rows.shape, 1)
    taps_down = jnp.where(lane < 64, rows_high, rows - rows_high).astype(jnp.bfloat16)
    for q in range(0, tiles, 2):
        down = jnp.dot(
            taps_down,
            pixels[:, q * LANES : (q + 2) * LANES],
            preferred_element_type=jnp.float32,
        )
        high, low = split_bf16(down)
        for t in range(n_terms):
            for h in range(2):
                for part, offset in ((high, 0), (low, 32)):
                    tile = part[t * 32 : t * 32 + 32, h * LANES : (h + 1) * LANES]
                    right = (q + h) * 64 + offset
                    windows[right : right + 32, (2 * t + 1) * LANES : (2 * t + 2) * LANES] = tile
                    windows[right + 64 : right + 96, 2 * t * LANES : (2 * t + 1) * LANES] = tile
    taps_across = jnp.concatenate([across_table[picks[t]] for t in range(n_terms)], axis=0)
    product = jnp.dot(windows[...], taps_across, preferred_element_type=jnp.float32)
    product = product[:, 0:LANES] + product[:, LANES : 2 * LANES]
    out = [product[c * 64 : c * 64 + 32] + product[c * 64 + 32 : c * 64 + 64] for c in range(tiles + 1)]
    lane = lax.broadcasted_iota(jnp.int32, out[0].shape, 1)
    out[0] = jnp.where(lane < LANES // 2, out[tiles], out[0])
    return jnp.concatenate(out[:tiles], axis=1).astype(jnp.bfloat16)


def match_kernel(
    dense, n_terms, taps,
    index_ref, coef_ref, start_ref, inverse_ref, blocks_ref, basis_ref, out_ref,
    pixels, windows, down_table, across_table,
):
    count = blocks_ref.shape[0]
    build_tables(basis_ref, down_table, across_table, basis_ref.shape[0], taps)
    pixels[...] = jnp.zeros_like(pixels)
    windows[...] = jnp.zeros_like(windows)
    if dense:
        out_ref[...] = jnp.zeros_like(out_ref)

    def body(step, carry):
        for k in range(2):
            b = step * 2 + k
            matched = match_block(
                b, index_ref, coef_ref, blocks_ref, pixels.at[k], windows.at[k],
                down_table, across_table, n_terms,
            )
            if dense:
                start = start_ref[b]
                first = jnp.minimum((start // 8) * 8, out_ref.shape[0] - 40)
                row = lax.broadcasted_iota(jnp.int32, (40, 32), 0)
                column = lax.broadcasted_iota(jnp.int32, (40, 32), 1)
                place = (row - column == start - first).astype(jnp.float32).astype(jnp.bfloat16)
                shifted = jnp.dot(place, matched, preferred_element_type=jnp.float32)
                out_ref[pl.ds(pl.multiple_of(first, 8), 40), :] += inverse_ref[b] * shifted
            else:
                out_ref[b] = matched
        return carry

    lax.fori_loop(0, count // 2, body, 0)


def match_all(blocks, picks, coef, starts, inverse, psf_basis, n_patch, dense):
    count, in_rows, columns = blocks.shape
    n_basis, _, taps = psf_basis.shape
    n_terms = picks.shape[0] // count
    half = (taps - 1) // 2
    tiles = columns // LANES
    down_line = jnp.pad(psf_basis[:, 0], ((0, 0), (0, 64 - taps)))
    down_line = jnp.concatenate([down_line, down_line], axis=1)
    tail = LANES - (LANES // 2 - half) - taps + 1
    across_line = jnp.pad(psf_basis[:, 1, ::-1], ((0, 0), (tail, LANES - taps - tail)))
    lines = jnp.stack([down_line, across_line], axis=1)
    if dense:
        out = jax.ShapeDtypeStruct((n_patch * PR, columns), jnp.float32)
    else:
        out = jax.ShapeDtypeStruct((count, in_rows - taps + 1, columns), jnp.bfloat16)
    smem = pl.BlockSpec(memory_space=pltpu.SMEM)
    vmem = pl.BlockSpec(memory_space=pltpu.VMEM)
    return pl.pallas_call(
        functools.partial(match_kernel, dense, n_terms, taps),
        out_shape=out,
        in_specs=[smem] * 4 + [vmem] * 2,
        out_specs=vmem,
        scratch_shapes=[
            pltpu.VMEM((2, 128, columns), jnp.bfloat16),
            pltpu.VMEM((2, (tiles + 1) * 64, n_terms * 2 * LANES), jnp.bfloat16),
            pltpu.VMEM((n_basis, 32, LANES), jnp.float32),
            pltpu.VMEM((n_basis, 2 * LANES, 2 * LANES), jnp.bfloat16),
        ],
        compiler_params=pltpu.CompilerParams(vmem_limit_bytes=VMEM_LIMIT),
    )(picks, coef, starts, inverse, blocks, lines)


def slots_route(matched, own_target, targets, row_offset, inverse, n_patch, own_patch):
    per_device = matched.shape[0]
    capacity = 2 * per_device // n_patch
    out_rows = matched.shape[1]
    positions = jnp.arange(per_device, dtype=jnp.int32)
    same_patch = targets[:, :, None] == targets[:, None, :]
    earlier = positions[None, :, None] > positions[None, None, :]
    slot_rank = jnp.sum(jnp.logical_and(same_patch, earlier), axis=2)
    peer_ids = jnp.arange(n_patch, dtype=jnp.int32)
    slot_ids = jnp.arange(capacity, dtype=jnp.int32)
    own_rank = lax.dynamic_slice_in_dim(slot_rank, own_patch, 1, 0)[0]
    source_pick = jnp.logical_and(
        own_target[None, None, :] == peer_ids[:, None, None],
        own_rank[None, None, :] == slot_ids[None, :, None],
    )
    source_index = jnp.sum(source_pick * positions[None, None, :], axis=2)
    present = jnp.any(source_pick, axis=2).astype(jnp.bfloat16)[:, :, None, None]
    taking = jnp.logical_and(
        targets[:, None, :] == own_patch, slot_rank[:, None, :] == slot_ids[None, :, None]
    )
    offsets_in = jnp.sum(taking * row_offset.reshape(n_patch, 1, per_device), axis=2)
    weights_in = jnp.sum(taking * inverse.reshape(n_patch, 1, per_device), axis=2)
    outgoing = matched[source_index] * present
    arrived = lax.all_to_all(outgoing, "patch", split_axis=0, concat_axis=0, tiled=True)
    slot_count = n_patch * capacity
    matched = arrived.reshape((slot_count,) + arrived.shape[2:])
    row_index = (
        offsets_in.reshape(slot_count)[:, None] + jnp.arange(out_rows, dtype=jnp.int32)[None, :]
    )
    placement = (row_index[None, :, :] == jnp.arange(PR, dtype=jnp.int32)[:, None, None]).astype(
        jnp.float32
    )
    placement = placement * weights_in.reshape(slot_count)[None, :, None]
    numerator = jnp.einsum(
        "rsi,siw->rw", placement, matched.astype(jnp.float32), precision=lax.Precision.HIGHEST
    )
    return lax.psum_scatter(numerator, "vgroup", scatter_dimension=0, tiled=True)


def swap_sum(keep, send, axis_name, pairs):
    got = lax.ppermute(send.astype(jnp.bfloat16), axis_name, pairs)
    return keep + got.astype(jnp.float32)


def dense_route(dense, own_patch, own_group, n_patch, n_group):
    columns = dense.shape[-1]
    sums = dense.reshape(n_patch, PR, columns)

    def flip(bit):
        return [(i, i ^ bit) for i in range(n_patch)]

    def cut(values, position, bit):
        mine = (own_patch // bit) % 2
        keep = lax.dynamic_index_in_dim(values, mine, position, keepdims=False)
        send = lax.dynamic_index_in_dim(values, 1 - mine, position, keepdims=False)
        return swap_sum(keep, send, "patch", flip(bit))

    sums = cut(sums.reshape(2, 2, 2, PR, columns), 2, 1)
    one = cut(cut(sums[:, :, : PR // 2], 1, 2), 0, 4)
    two = cut(cut(sums[:, :, PR // 2 :], 0, 4), 0, 2)
    sums = jnp.concatenate([one, two], axis=0).reshape(n_group, PR // n_group, columns)
    total = lax.dynamic_index_in_dim(sums, own_group, 0, keepdims=False)
    for shift in range(1, n_group):
        pairs = [(i, (i + shift) % n_group) for i in range(n_group)]
        send = lax.dynamic_index_in_dim(sums, (own_group + shift) % n_group, 0, keepdims=False)
        total = swap_sum(total, send, "vgroup", pairs)
    return total


def local(exposures, target_patch, row_offset, basis_index, basis_coef, inv_variance, psf_basis):
    n_patch, n_group = lax.axis_size("patch"), lax.axis_size("vgroup")
    own_patch, own_group = lax.axis_index("patch"), lax.axis_index("vgroup")
    blocks = exposures[0]
    per_device, in_rows, columns = blocks.shape
    taps = psf_basis.shape[-1]
    out_rows = in_rows - taps + 1
    share = PR // n_group
    dense = n_patch == 8 and n_patch * PR * columns * 4 <= DENSE_LIMIT

    def own(values):
        return lax.dynamic_slice_in_dim(values, own_patch * per_device, per_device, 0)

    all_starts = target_patch[0, :, 0] * PR + row_offset[0]
    starts, inverse = own(all_starts), own(inv_variance[0])
    picks, coef = own(basis_index[0]).reshape(-1), own(basis_coef[0]).reshape(-1)

    spread = jnp.stack([all_starts.astype(jnp.float32), inv_variance[0]])
    spread = lax.all_gather(spread, "vgroup", axis=0, tiled=False)
    first = own_patch * PR + own_group * share
    rows = (first + jnp.arange(share, dtype=jnp.int32)).astype(jnp.float32)[:, None, None]
    inside = jnp.logical_and(rows >= spread[None, :, 0], rows < spread[None, :, 0] + out_rows)
    weight = jnp.sum(jnp.where(inside, spread[None, :, 1], 0.0), axis=(1, 2))

    result = match_all(blocks, picks, coef, starts, inverse, psf_basis, n_patch, dense)
    if dense:
        numerator = dense_route(result, own_patch, own_group, n_patch, n_group)
    else:
        targets = target_patch[0, :, 0].reshape(n_patch, per_device)
        own_target = lax.dynamic_slice_in_dim(targets, own_patch, 1, 0)[0]
        numerator = slots_route(
            result, own_target, targets, row_offset[0], inv_variance[0], n_patch, own_patch
        )
    coadd = jnp.roll(numerator / (1.0 + weight[:, None]), -(LANES // 2), axis=1)
    return (coadd, weight)


def solution(mesh):
    in_specs = (
        P("vgroup", "patch", None, None),
        P("vgroup", None, None),
        P("vgroup", None),
        P("vgroup", None, None),
        P("vgroup", None, None),
        P("vgroup", None),
        P(),
    )
    out_specs = (P(("patch", "vgroup"), None), P(("patch", "vgroup")))
    return jax.shard_map(local, mesh=mesh, in_specs=in_specs, out_specs=out_specs, check_vma=False)
```

time: 1250 us -> 179 us (0.14)
  other arithmetic: 1030 us -> 16.7 us
  waiting for transfers between devices: 120 us -> 47.3 us
  Pallas kernels: 0 us -> 56.4 us
  between operations: 15 us -> 0.88 us
    add x26 -> x8, other arithmetic: 617 us -> 12.9 us  [the longest x5 12.2 us: swap_sum(): return keep + got.astype(jnp.float32)]
    dynamic_update_slice x8 -> x0, other arithmetic: 377 us -> none  [match_all(): matched = lax.map(lambda members: psf_match(*members), shaped)]
    all_to_all x1 -> x0, waiting for transfers between devices: 91.9 us -> none  [local(): lax.all_to_all(outgoing, 'patch', split_axis=0, concat_axis=0, tiled=True)]
    pallas_call x0 -> x1, Pallas kernels: none -> 56.4 us  [match_all(): pl.pallas_call(functools.partial(match_kernel, dense, n_terms, taps), out...]
    ppermute x0 -> x8, waiting for transfers between devices: none -> 47.3 us  [swap_sum(): got = lax.ppermute(send.astype(jnp.bfloat16), axis_name, pairs)]
    reduce_scatter x1 -> x0, waiting for transfers between devices: 28.3 us -> none  [local(): lax.psum_scatter(numerator, 'vgroup', scatter_dimension=0, tiled=True)]
    convert_element_type x9 -> x2, other arithmetic: 22.7 us -> 0.01 us  [the longest x1 0.01 us: local(): spread = jnp.stack([all_starts.astype(jnp.float32), inv_variance[0]])]
    mul x83 -> x0, local copies, waits for them, and re-layouts: 13.1 us -> none  [the longest x1 12.1 us: local(): outgoing = matched_own[source_index] * present]
  transfers between devices with their start and end apart: 2 -> 8, of which waited for: 2 -> 7; matrix products, arithmetic and copies ran while one was open for 0% -> 4% of each run, Pallas kernels for 0% -> 0%
where the time goes in v1:
time: 179 us; the launch traced here: 177 us
  Pallas kernels  56.4 us (32%)
  waiting for transfers between devices  47.3 us (26%)
  local copies, waits for them, and re-layouts  32.3 us (18%)
  other arithmetic  16.7 us (9%)
  blocking collectives  12.1 us (7%)
  starting transfers between devices  11.4 us (6%)
    pallas_call x1, Pallas kernels, match_all(): pl.pallas_call(functools.partial(match_kernel, dense, n_terms, taps), out...  56.4 us
    ppermute x8, waiting for transfers between devices, swap_sum(): got = lax.ppermute(send.astype(jnp.bfloat16), axis_name, pairs)  47.3 us
    unnamed x22, local copies, waits for them, and re-layouts  15.2 us
    add x5, other arithmetic, swap_sum(): return keep + got.astype(jnp.float32)  12.2 us
    all_gather x1, blocking collectives, local(): spread = lax.all_gather(spread, 'vgroup', axis=0, tiled=False)  12.1 us
    ppermute x8, starting transfers between devices, swap_sum(): got = lax.ppermute(send.astype(jnp.bfloat16), axis_name, pairs)  11.4 us
    convert_element_type x6, local copies, waits for them, and re-layouts, swap_sum(): got = lax.ppermute(send.astype(jnp.bfloat16), axis_name, pairs)  8.93 us
  transfers between devices with their start and end apart: 8, of which 7 were waited for; matrix products, arithmetic and copies ran while one was open for 4% of the time, Pallas kernels for 0%

profile of v1, /device:TPU:0, one launch (start us, length us, event | category | flops | bytes accessed | tf_op | source)
XLA Modules:
  0.0 177.0 jit_solution(10909951690116684235)
XLA Ops:
  0.7 0.7 copy-done
  1.5 0.6 reshape.58.index_ref
  2.1 0.8 constant_dynamic-slice_fusion.1
  2.9 0.7 reshape.59.coef_ref
  3.6 0.7 broadcast_multiply_fusion
  4.3 0.7 add.151
  5.0 0.6 dynamic_slice.63.start_ref
  5.6 1.2 fusion.12.inverse_ref
  6.8 0.9 fusion.14
  7.7 0.1 copy.35
  7.9 0.1 copy.36
  8.1 11.0 %copy.45 = bf16[1,32,62,2048]{3,2,1,0:T(8,128)(2,1)} copy(bf16[1,32,62,2048]{3,1,2,0:T(8,128)(2,1)} %param.7) | data formatting | bytes 16252928 | tf_op args[0]
  19.2 0.7 pad_maximum_fusion.2.basis_ref
  19.8 56.4 %shard_map.86 = f32[2048,2048]{1,0:T(8,128)} custom-call(s32[96]{0:T(128)} %reshape.58.index_ref, f32[96]{0:T(128)} %reshape.59.coef_ref, s32[32]{0:T(128)} %dynamic_slice.63.start_ref, f32[32]{0:T(128)} %fusion.12.inverse_ref, bf16[32,62,2048]{2,1,0:T(8,128)(2,1)} %bitcast.65, f32[35,2,128]{2,1,0:T(2,128)} %pad_maximum_fusion.2.basis_ref), custom_call_target="tpu_custom_call" | custom-call | tf_op jit(solution)/shard_map/pallas_call | solution.py:135
  76.2 6.0 %fusion = bf16[2,2,256,2048]{3,2,1,0:T(8,128)(2,1)} fusion(f32[2,2,2,256,2048]{4,3,2,1,0:T(8,128)} %bitcast.63, s32[]{:T(128)S(6)} %select_n.93), kind=kLoop, calls=%fused_computation.3 | loop fusion | bytes 8388612 | tf_op jit(solution)/shard_map/convert_element_type | solution.py:190
  82.2 0.5 collective-permute-start
  82.7 7.1 %collective-permute-done = bf16[2,2,256,2048]{3,2,1,0:T(8,128)(2,1)} collective-permute-done((bf16[2,2,256,2048]{3,2,1,0:T(8,128)(2,1)}, bf16[2,2,256,2048]{3,2,1,0:T(8,128)(2,1)}, u32[]{:S(2)}, u32[]{:S(2)}) %collective-permute-start) | collective-permute-done | bytes 4194336 | tf_op jit(solution)/shard_map/ppermute | solution.py:190
  89.8 5.9 %bitcast_add_fusion = f32[2,2,256,2048]{3,2,1,0:T(8,128)S(1)} fusion(bf16[2,2,256,2048]{3,2,1,0:T(8,128)(2,1)} %collective-permute-done, f32[2,2,2,256,2048]{4,3,2,1,0:T(8,128)} %bitcast.64, s32[]{:T(128)S(6)} %select_n.92), kind=kLoop, calls=%fused_computation | loop fusion | flops 4194304 | bytes 20971524 | tf_op jit(solution)/shard_map/add | solution.py:191
  95.8 2.7 %fusion.13 = (f32[2,2,128,2048]{3,2,1,0:T(8,128)S(1)}, f32[2,2,128,2048]{3,2,1,0:T(8,128)}) fusion(f32[2,2,256,2048]{3,2,1,0:T(8,128)S(1)} %bitcast_add_fusion), kind=kLoop, calls=%fused_computation.44 | loop fusion | bytes 16777216 | tf_op jit(solution)/shard_map/slice | solution.py:208
  98.5 2.0 %copy-done.3 = f32[2,2,128,2048]{3,2,1,0:T(8,128)} copy-done((f32[2,2,128,2048]{3,2,1,0:T(8,128)}, f32[2,2,128,2048]{3,2,1,0:T(8,128)S(1)}, u32[]{:S(2)}) %copy-start.3) | copy-done | bytes 4194328
  100.5 0.1 fusion.2
  100.6 2.9 %collective-permute-start.1 = (bf16[2,128,2048]{2,1,0:T(8,128)(2,1)S(1)}, bf16[2,128,2048]{2,1,0:T(8,128)(2,1)}, u32[]{:S(2)}, u32[]{:S(2)}) collective-permute-start(bf16[2,128,2048]{2,1,0:T(8,128)(2,1)S(1)} %fusion.2), channel_id=1, source_target_pairs={{0,8},{4,12},{8,0},{12,4},{16,24},{20,28},{24,16},{28,20},{1,9},{5... | collective-permute-start | bytes 3145736 | tf_op jit(solution)/shard_map/ppermute | solution.py:190
  103.6 12.1 %all-gather.1 = f32[4,2,256]{2,1,0:T(2,128)S(1)} all-gather(f32[1,2,256]{2,1,0:T(2,128)S(1)} %maximum_bitcast_fusion), channel_id=2, replica_groups=mesh['patch'=8,'vgroup'=4] {'vgroup'}, dimensions={0}, use_global_device_ids=true | all-gather | bytes 10240 | tf_op jit(solution)/shard_map/all_gather | solution.py:237
  115.7 1.7 fusion.1
  117.5 1.6 collective-permute-start.3
  119.1 8.0 %collective-permute-done.1 = bf16[2,128,2048]{2,1,0:T(8,128)(2,1)} collective-permute-done((bf16[2,128,2048]{2,1,0:T(8,128)(2,1)S(1)}, bf16[2,128,2048]{2,1,0:T(8,128)(2,1)}, u32[]{:S(2)}, u32[]{:S(2)}) %collective-permute-start.1) | collective-permute-done | bytes 1048608 | tf_op jit(solution)/shard_map/ppermute | solution.py:190
  127.1 2.2 %bitcast_add_fusion.1 = f32[2,128,2048]{2,1,0:T(8,128)S(1)} fusion(bf16[2,128,2048]{2,1,0:T(8,128)(2,1)} %collective-permute-done.1, f32[2,2,128,2048]{3,2,1,0:T(8,128)} %copy-done.3, s32[]{:T(128)S(6)} %select_n.96), kind=kLoop, calls=%fused_computation.6 | loop fusion | flops 1048576 | bytes 5242884 | tf_op jit(solution)/shard_map/add | solution.py:191
  129.3 0.9 fusion.3
  130.2 1.8 collective-permute-start.2
  131.9 11.8 %collective-permute-done.3 = bf16[2,128,2048]{2,1,0:T(8,128)(2,1)} collective-permute-done((bf16[2,128,2048]{2,1,0:T(8,128)(2,1)S(1)}, bf16[2,128,2048]{2,1,0:T(8,128)(2,1)}, u32[]{:S(2)}, u32[]{:S(2)}) %collective-permute-start.3) | collective-permute-done | bytes 1048608 | tf_op jit(solution)/shard_map/ppermute | solution.py:190
  143.8 1.6 bitcast_add_fusion.2
  145.4 1.3 copy-done.4
  146.8 0.6 collective-permute-start.4
  147.4 4.2 %collective-permute-done.2 = bf16[128,2048]{1,0:T(8,128)(2,1)} collective-permute-done((bf16[128,2048]{1,0:T(8,128)(2,1)}, bf16[128,2048]{1,0:T(8,128)(2,1)}, u32[]{:S(2)}, u32[]{:S(2)}) %collective-permute-start.2) | collective-permute-done | bytes 524320 | tf_op jit(solution)/shard_map/ppermute | solution.py:190
  151.6 1.2 bitcast_add_fusion.4
  152.8 3.2 %collective-permute-done.4 = bf16[128,2048]{1,0:T(8,128)(2,1)S(1)} collective-permute-done((bf16[128,2048]{1,0:T(8,128)(2,1)S(1)}, bf16[128,2048]{1,0:T(8,128)(2,1)S(1)}, u32[]{:S(2)}, u32[]{:S(2)}) %collective-permute-start.4) | collective-permute-done | bytes 524320 | tf_op jit(solution)/shard_map/ppermute | solution.py:190
  156.0 1.4 bitcast_add_fusion.3
  157.4 0.1 pad_maximum_fusion
  157.5 0.1 fusion.8
  157.6 1.6 collective-permute-start.5
  159.3 1.1 collective-permute-start.6
  160.4 1.3 collective-permute-start.7
  161.7 0.2 select_reduce_fusion
  161.9 5.2 %collective-permute-done.5 = bf16[64,2048]{1,0:T(8,128)(2,1)S(1)} collective-permute-done((bf16[64,2048]{1,0:T(8,128)(2,1)S(1)}, bf16[64,2048]{1,0:T(8,128)(2,1)S(1)}, u32[]{:S(2)}, u32[]{:S(2)}) %collective-permute-start.5) | collective-permute-done | bytes 262176 | tf_op jit(solution)/shard_map/ppermute | solution.py:190
  167.1 7.7 %collective-permute-done.6 = bf16[64,2048]{1,0:T(8,128)(2,1)S(1)} collective-permute-done((bf16[64,2048]{1,0:T(8,128)(2,1)S(1)}, bf16[64,2048]{1,0:T(8,128)(2,1)S(1)}, u32[]{:S(2)}, u32[]{:S(2)}) %collective-permute-start.6) | collective-permute-done | bytes 262176 | tf_op jit(solution)/shard_map/ppermute | solution.py:190
  174.8 1.1 fusion.7
  175.9 0.2 slice.39
  176.1 0.9 pad_maximum_fusion.1
  (34 shorter events, 0.7 us)
Async XLA Ops:
  0.6 0.7 copy-start
  82.2 7.6 %collective-permute-start = (bf16[2,2,256,2048]{3,2,1,0:T(8,128)(2,1)}, bf16[2,2,256,2048]{3,2,1,0:T(8,128)(2,1)}, u32[]{:S(2)}, u32[]{:S(2)}) collective-permute-start(bf16[2,2,256,2048]{3,2,1,0:T(8,128)(2,1)} %fusion), channel_id=1, source_target_pairs={{0,4},{4,0},{8,12},{12,8},{16,20},{20,16},{24,28},{28,24},{1,5},{5... | collective-permute-start | bytes 12582920 | tf_op jit(solution)/shard_map/ppermute | solution.py:190
  95.7 7.8 %copy-start.5 = (s32[1,256]{1,0:T(1,128)S(1)}, s32[1,256]{1,0:T(1,128)}, u32[]{:S(2)}) copy-start(s32[1,256]{1,0:T(1,128)} %param.9) | copy-start | bytes 3076
  95.7 7.8 %copy-start.6 = (s32[1,256,1]{1,2,0:T(1,128)S(1)}, s32[1,256,1]{1,2,0:T(1,128)}, u32[]{:S(2)}) copy-start(s32[1,256,1]{1,2,0:T(1,128)} %param.8) | copy-start | bytes 3076
  95.8 7.8 %copy-start.7 = (f32[1,256]{1,0:T(1,128)S(1)}, f32[1,256]{1,0:T(1,128)}, u32[]{:S(2)}) copy-start(f32[1,256]{1,0:T(1,128)} %param.12) | copy-start | bytes 3076
  98.5 2.0 %copy-start.3 = (f32[2,2,128,2048]{3,2,1,0:T(8,128)}, f32[2,2,128,2048]{3,2,1,0:T(8,128)S(1)}, u32[]{:S(2)}) copy-start(f32[2,2,128,2048]{3,2,1,0:T(8,128)S(1)} %get-tuple-element.2) | copy-start | bytes 12582916
  100.6 26.5 %collective-permute-start.1 = (bf16[2,128,2048]{2,1,0:T(8,128)(2,1)S(1)}, bf16[2,128,2048]{2,1,0:T(8,128)(2,1)}, u32[]{:S(2)}, u32[]{:S(2)}) collective-permute-start(bf16[2,128,2048]{2,1,0:T(8,128)(2,1)S(1)} %fusion.2), channel_id=1, source_target_pairs={{0,8},{4,12},{8,0},{12,4},{16,24},{20,28},{24,16},{28,20},{1,9},{5... | collective-permute-start | bytes 3145736 | tf_op jit(solution)/shard_map/ppermute | solution.py:190
  117.5 26.3 %collective-permute-start.3 = (bf16[2,128,2048]{2,1,0:T(8,128)(2,1)S(1)}, bf16[2,128,2048]{2,1,0:T(8,128)(2,1)}, u32[]{:S(2)}, u32[]{:S(2)}) collective-permute-start(bf16[2,128,2048]{2,1,0:T(8,128)(2,1)S(1)} %fusion.1), channel_id=1, source_target_pairs={{0,16},{4,20},{8,24},{12,28},{16,0},{20,4},{24,8},{28,12},{1,17},{... | collective-permute-start | bytes 3145736 | tf_op jit(solution)/shard_map/ppermute | solution.py:190
  119.1 24.7 %copy-start.2 = (f32[2,2,128,2048]{3,2,1,0:T(8,128)S(1)}, f32[2,2,128,2048]{3,2,1,0:T(8,128)}, u32[]{:S(2)}) copy-start(f32[2,2,128,2048]{3,2,1,0:T(8,128)} %get-tuple-element.3) | copy-start | bytes 12582916
  130.2 21.5 %collective-permute-start.2 = (bf16[128,2048]{1,0:T(8,128)(2,1)}, bf16[128,2048]{1,0:T(8,128)(2,1)}, u32[]{:S(2)}, u32[]{:S(2)}) collective-permute-start(bf16[128,2048]{1,0:T(8,128)(2,1)} %fusion.3), channel_id=1, source_target_pairs={{0,16},{4,20},{8,24},{12,28},{16,0},{20,4},{24,8},{28,12},{1,17},{... | collective-permute-start | bytes 1572872 | tf_op jit(solution)/shard_map/ppermute | solution.py:190
  145.4 1.3 copy-start.4
  146.8 9.2 %collective-permute-start.4 = (bf16[128,2048]{1,0:T(8,128)(2,1)S(1)}, bf16[128,2048]{1,0:T(8,128)(2,1)S(1)}, u32[]{:S(2)}, u32[]{:S(2)}) collective-permute-start(bf16[128,2048]{1,0:T(8,128)(2,1)S(1)} %fusion.4), channel_id=1, source_target_pairs={{0,8},{4,12},{8,0},{12,4},{16,24},{20,28},{24,16},{28,20},{1,9},{5... | collective-permute-start | bytes 1572872 | tf_op jit(solution)/shard_map/ppermute | solution.py:190
  156.0 21.0 %copy-start.1 = (s32[1,256,3]{1,0,2:T(1,128)S(1)}, s32[1,256,3]{1,0,2:T(1,128)}, u32[]{:S(2)}) copy-start(s32[1,256,3]{1,0,2:T(1,128)} %param.10) | copy-start | bytes 9220
  157.6 9.4 %collective-permute-start.5 = (bf16[64,2048]{1,0:T(8,128)(2,1)S(1)}, bf16[64,2048]{1,0:T(8,128)(2,1)S(1)}, u32[]{:S(2)}, u32[]{:S(2)}) collective-permute-start(bf16[64,2048]{1,0:T(8,128)(2,1)S(1)} %get-tuple-element.4), channel_id=1, source_target_pairs={{0,1},{1,2},{2,3},{3,0},{4,5},{5,6},{6,7},{7,4},{8,9},{9,10},{10,1... | collective-permute-start | bytes 786440 | tf_op jit(solution)/shard_map/ppermute | solution.py:190
  159.3 15.5 %collective-permute-start.6 = (bf16[64,2048]{1,0:T(8,128)(2,1)S(1)}, bf16[64,2048]{1,0:T(8,128)(2,1)S(1)}, u32[]{:S(2)}, u32[]{:S(2)}) collective-permute-start(bf16[64,2048]{1,0:T(8,128)(2,1)S(1)} %get-tuple-element.6), channel_id=1, source_target_pairs={{0,2},{1,3},{2,0},{3,1},{4,6},{5,7},{6,4},{7,5},{8,10},{9,11},{10,... | collective-permute-start | bytes 786440 | tf_op jit(solution)/shard_map/ppermute | solution.py:190
  160.4 14.4 %collective-permute-start.7 = (bf16[64,2048]{1,0:T(8,128)(2,1)S(1)}, bf16[64,2048]{1,0:T(8,128)(2,1)}, u32[]{:S(2)}, u32[]{:S(2)}) collective-permute-start(bf16[64,2048]{1,0:T(8,128)(2,1)S(1)} %get-tuple-element.5), channel_id=1, source_target_pairs={{0,3},{1,0},{2,1},{3,2},{4,7},{5,4},{6,5},{7,6},{8,11},{9,8},{10,9... | collective-permute-start | bytes 786440 | tf_op jit(solution)/shard_map/ppermute | solution.py:190
  161.9 15.1 %copy-start.8 = (f32[64]{0:T(128)}, f32[64]{0:T(128)S(1)}, u32[]{:S(2)}) copy-start(f32[64]{0:T(128)S(1)} %select_reduce_fusion) | copy-start | bytes 772

commit v2 on v1

--- a/solution.py
+++ b/solution.py
@@ -186,45 +186,168 @@
     return lax.psum_scatter(numerator, "vgroup", scatter_dimension=0, tiled=True)
 
 
-def swap_sum(keep, send, axis_name, pairs):
-    got = lax.ppermute(send.astype(jnp.bfloat16), axis_name, pairs)
-    return keep + got.astype(jnp.float32)
-
-
-def dense_route(dense, own_patch, own_group, n_patch, n_group):
+def route_kernel(
+    chunks, dense_ref, weight_ref, total_ref, weight_out_ref,
+    send_core, got_core, send_one, got_one, keep_one, send_two, got_two, keep_two,
+    send_group, got_group, got_weight,
+    core_sems, one_sems, two_sems, group_sems, weight_sems,
+):
+    p, z = lax.axis_index("patch"), lax.axis_index("vgroup")
+    n_group = dense_ref.shape[3]
+    half = n_group // 2
+    width = dense_ref.shape[-1] // chunks
+    y, x, c = p // 4, (p // 2) % 2, p % 2
+    across_core = (p + 1 - 2 * c, z)
+    across_x = (p + 2 - 4 * x, z)
+    across_y = (p + 4 - 8 * y, z)
+    groups = [(z + d) % n_group for d in range(1, n_group)]
+    across_z = [(p, to) for to in groups]
+
+    barrier = pltpu.get_barrier_semaphore()
+    partners = [across_core, across_x, across_y] + across_z
+    for partner in partners:
+        pl.semaphore_signal(barrier, inc=1, device_id=partner, device_id_type=pl.DeviceIdType.MESH)
+    pl.semaphore_wait(barrier, len(partners))
+
+    copies = []
+
+    def go(source, target, sems, place, device):
+        copy = pltpu.make_async_remote_copy(
+            src_ref=source, dst_ref=target,
+            send_sem=sems.at[(0,) + place], recv_sem=sems.at[(1,) + place],
+            device_id=device, device_id_type=pl.DeviceIdType.MESH,
+        )
+        copy.start()
+        copies.append(copy)
+        return copy
+
+    def wide(values):
+        return values.astype(jnp.float32)
+
+    core_copies, one_copies, two_copies, group_copies = {}, {}, {}, {}
+
+    def stage_core(g):
+        cols = slice(g * width, (g + 1) * width)
+        send_core[g] = dense_ref[:, :, 1 - c, :, :, cols].astype(jnp.bfloat16)
+        core_copies[g] = go(send_core.at[g], got_core.at[g], core_sems, (g,), across_core)
+
+    def stage_one(g):
+        cols = slice(g * width, (g + 1) * width)
+        core_copies[g].wait_recv()
+        low, high = slice(0, half), slice(half, n_group)
+        send_one[g, 0] = (
+            dense_ref[:, 1 - x, c, low, :, cols] + wide(got_core[g, :, 1 - x, low])
+        ).astype(jnp.bfloat16)
+        first = go(send_one.at[g, 0], got_one.at[g, 0], one_sems, (g, 0), across_x)
+        send_one[g, 1] = (
+            dense_ref[1 - y, :, c, high, :, cols] + wide(got_core[g, 1 - y, :, high])
+        ).astype(jnp.bfloat16)
+        second = go(send_one.at[g, 1], got_one.at[g, 1], one_sems, (g, 1), across_y)
+        keep_one[g, 0] = dense_ref[:, x, c, low, :, cols] + wide(got_core[g, :, x, low])
+        keep_one[g, 1] = dense_ref[y, :, c, high, :, cols] + wide(got_core[g, y, :, high])
+        one_copies[g] = (first, second)
+
+    def stage_two(g):
+        pair = []
+        for h, (side, device) in enumerate(((y, across_y), (x, across_x))):
+            one_copies[g][h].wait_recv()
+            send_two[g, h] = (keep_one[g, h, 1 - side] + wide(got_one[g, h, 1 - side])).astype(
+                jnp.bfloat16
+            )
+            pair.append(go(send_two.at[g, h], got_two.at[g, h], two_sems, (g, h), device))
+            keep_two[g, h * half : (h + 1) * half] = keep_one[g, h, side] + wide(
+                got_one[g, h, side]
+            )
+        two_copies[g] = pair
+
+    def stage_group(g):
+        for h in range(2):
+            two_copies[g][h].wait_recv()
+            part = slice(h * half, (h + 1) * half)
+            keep_two[g, part] = keep_two[g, part] + wide(got_two[g, h])
+        sent = []
+        for d, to in enumerate(groups):
+            send_group[g, d] = keep_two[g, to].astype(jnp.bfloat16)
+            sent.append(
+                go(send_group.at[g, d], got_group.at[g, d], group_sems, (g, d), across_z[d])
+            )
+        group_copies[g] = sent
+
+    def stage_end(g):
+        total = keep_two[g, z]
+        for d in range(n_group - 1):
+            group_copies[g][d].wait_recv()
+            total = total + wide(got_group[g, d])
+        total_ref[:, g * width : (g + 1) * width] = total
+
+    weight_copies = [
+        go(weight_ref.at[to], got_weight.at[d], weight_sems, (d,), across_z[d])
+        for d, to in enumerate(groups)
+    ]
+    for g in range(chunks):
+        stage_core(g)
+    stages = (stage_one, stage_two, stage_group, stage_end)
+    for step in range(chunks + len(stages) - 1):
+        for late, stage in enumerate(stages):
+            if 0 <= step - late < chunks:
+                stage(step - late)
+    total = weight_ref[z]
+    for d in range(n_group - 1):
+        weight_copies[d].wait_recv()
+        total = total + got_weight[d]
+    weight_out_ref[...] = total
+    for copy in copies:
+        copy.wait_send()
+
+
+def dense_route(dense, weight, n_group):
     columns = dense.shape[-1]
-    sums = dense.reshape(n_patch, PR, columns)
-
-    def flip(bit):
-        return [(i, i ^ bit) for i in range(n_patch)]
-
-    def cut(values, position, bit):
-        mine = (own_patch // bit) % 2
-        keep = lax.dynamic_index_in_dim(values, mine, position, keepdims=False)
-        send = lax.dynamic_index_in_dim(values, 1 - mine, position, keepdims=False)
-        return swap_sum(keep, send, "patch", flip(bit))
-
-    sums = cut(sums.reshape(2, 2, 2, PR, columns), 2, 1)
-    one = cut(cut(sums[:, :, : PR // 2], 1, 2), 0, 4)
-    two = cut(cut(sums[:, :, PR // 2 :], 0, 4), 0, 2)
-    sums = jnp.concatenate([one, two], axis=0).reshape(n_group, PR // n_group, columns)
-    total = lax.dynamic_index_in_dim(sums, own_group, 0, keepdims=False)
-    for shift in range(1, n_group):
-        pairs = [(i, (i + shift) % n_group) for i in range(n_group)]
-        send = lax.dynamic_index_in_dim(sums, (own_group + shift) % n_group, 0, keepdims=False)
-        total = swap_sum(total, send, "vgroup", pairs)
-    return total
+    share = PR // n_group
+    half = n_group // 2
+    chunks = 4
+    width = columns // chunks
+    peers = n_group - 1
+    vmem = pl.BlockSpec(memory_space=pltpu.VMEM)
+    dense = dense.reshape(2, 2, 2, n_group, share, columns)
+    weight = jnp.pad(weight.reshape(n_group, 1, share), ((0, 0), (0, 0), (0, LANES - share)))
+    weight = jnp.broadcast_to(weight, (n_group, 8, LANES))
+
+    def buffer(*dims, kind=jnp.bfloat16):
+        return pltpu.VMEM((chunks,) + dims + (share, width), kind)
+
+    sems = pltpu.SemaphoreType.DMA
+    total, weight = pl.pallas_call(
+        functools.partial(route_kernel, chunks),
+        out_shape=(
+            jax.ShapeDtypeStruct((share, columns), jnp.float32),
+            jax.ShapeDtypeStruct((8, LANES), jnp.float32),
+        ),
+        in_specs=[vmem] * 2,
+        out_specs=(vmem, vmem),
+        scratch_shapes=[
+            buffer(2, 2, n_group), buffer(2, 2, n_group),
+            buffer(2, 2, half), buffer(2, 2, half), buffer(2, 2, half, kind=jnp.float32),
+            buffer(2, half), buffer(2, half), buffer(n_group, kind=jnp.float32),
+            buffer(peers), buffer(peers),
+            pltpu.VMEM((peers, 8, LANES), jnp.float32),
+            sems((2, chunks)), sems((2, chunks, 2)), sems((2, chunks, 2)),
+            sems((2, chunks, peers)), sems((2, peers)),
+        ],
+        compiler_params=pltpu.CompilerParams(
+            collective_id=0, has_side_effects=True, vmem_limit_bytes=VMEM_LIMIT
+        ),
+    )(dense, weight)
+    return total, weight[0, :share]
 
 
 def local(exposures, target_patch, row_offset, basis_index, basis_coef, inv_variance, psf_basis):
     n_patch, n_group = lax.axis_size("patch"), lax.axis_size("vgroup")
-    own_patch, own_group = lax.axis_index("patch"), lax.axis_index("vgroup")
+    own_patch = lax.axis_index("patch")
     blocks = exposures[0]
     per_device, in_rows, columns = blocks.shape
     taps = psf_basis.shape[-1]
     out_rows = in_rows - taps + 1
-    share = PR // n_group
-    dense = n_patch == 8 and n_patch * PR * columns * 4 <= DENSE_LIMIT
+    dense = n_patch == 8 and n_group % 2 == 0 and n_patch * PR * columns * 4 <= DENSE_LIMIT
 
     def own(values):
         return lax.dynamic_slice_in_dim(values, own_patch * per_device, per_device, 0)
@@ -233,22 +356,20 @@
     starts, inverse = own(all_starts), own(inv_variance[0])
     picks, coef = own(basis_index[0]).reshape(-1), own(basis_coef[0]).reshape(-1)
 
-    spread = jnp.stack([all_starts.astype(jnp.float32), inv_variance[0]])
-    spread = lax.all_gather(spread, "vgroup", axis=0, tiled=False)
-    first = own_patch * PR + own_group * share
-    rows = (first + jnp.arange(share, dtype=jnp.int32)).astype(jnp.float32)[:, None, None]
-    inside = jnp.logical_and(rows >= spread[None, :, 0], rows < spread[None, :, 0] + out_rows)
-    weight = jnp.sum(jnp.where(inside, spread[None, :, 1], 0.0), axis=(1, 2))
+    rows = (own_patch * PR + jnp.arange(PR, dtype=jnp.int32))[:, None]
+    inside = jnp.logical_and(rows >= all_starts[None], rows < all_starts[None] + out_rows)
+    weight = jnp.sum(jnp.where(inside, inv_variance[0][None], 0.0), axis=1)
 
     result = match_all(blocks, picks, coef, starts, inverse, psf_basis, n_patch, dense)
     if dense:
-        numerator = dense_route(result, own_patch, own_group, n_patch, n_group)
+        numerator, weight = dense_route(result, weight, n_group)
     else:
         targets = target_patch[0, :, 0].reshape(n_patch, per_device)
         own_target = lax.dynamic_slice_in_dim(targets, own_patch, 1, 0)[0]
         numerator = slots_route(
             result, own_target, targets, row_offset[0], inv_variance[0], n_patch, own_patch
         )
+        weight = lax.psum_scatter(weight, "vgroup", scatter_dimension=0, tiled=True)
     coadd = jnp.roll(numerator / (1.0 + weight[:, None]), -(LANES // 2), axis=1)
     return (coadd, weight)
 

time: 179 us -> 141 us (0.79)
  Pallas kernels: 56.4 us -> 116 us
  waiting for transfers between devices: 47.3 us -> 0 us
  local copies, waits for them, and re-layouts: 32.3 us -> 18.1 us
  blocking collectives: 12.1 us -> 0 us
  starting transfers between devices: 11.4 us -> 0 us
  other arithmetic: 16.7 us -> 5.49 us
    pallas_call x0 -> x1, Pallas kernels: none -> 59.9 us  [dense_route(): pl.pallas_call(functools.partial(route_kernel, chunks), out_shape=(jax.Sh...]
    ppermute x8 -> x0, waiting for transfers between devices: 47.3 us -> none  [swap_sum(): got = lax.ppermute(send.astype(jnp.bfloat16), axis_name, pairs)]
    add x6 -> x2, other arithmetic: 12.2 us -> 0.01 us  [the longest x1 0.01 us: local(): all_starts[None] + out_rows]
    all_gather x1 -> x0, blocking collectives: 12.1 us -> none  [local(): spread = lax.all_gather(spread, 'vgroup', axis=0, tiled=False)]
    ppermute x8 -> x0, starting transfers between devices: 11.4 us -> none  [swap_sum(): got = lax.ppermute(send.astype(jnp.bfloat16), axis_name, pairs)]
    convert_element_type x6 -> x0, local copies, waits for them, and re-layouts: 8.93 us -> none  [swap_sum(): got = lax.ppermute(send.astype(jnp.bfloat16), axis_name, pairs)]
    unnamed x22 -> x11, local copies, waits for them, and re-layouts: 15.2 us -> 11.9 us
    slice x2 -> x0, local copies, waits for them, and re-layouts: 2.74 us -> none  [the longest x1 2.73 us: dense_route(): one = cut(cut(sums[:, :, :PR // 2], 1, 2), 0, 4)]
  transfers between devices with their start and end apart: 8 -> 0, of which waited for: 7 -> 0; matrix products, arithmetic and copies ran while one was open for 4% -> 0% of each run, Pallas kernels for 0% -> 0%
where the time goes in v2:
time: 141 us
  Pallas kernels  116 us (82%)
  local copies, waits for them, and re-layouts  18.1 us (13%)
  other arithmetic  5.49 us (4%)
    pallas_call x1, Pallas kernels, dense_route(): pl.pallas_call(functools.partial(route_kernel, chunks), out_shape=(jax.Sh...  59.9 us
    pallas_call x1, Pallas kernels, match_all(): pl.pallas_call(functools.partial(match_kernel, dense, n_terms, taps), out...  56.4 us
    unnamed x11, local copies, waits for them, and re-layouts  11.9 us
    dynamic_slice x6, local copies, waits for them, and re-layouts, own(): lax.dynamic_slice_in_dim(values, own_patch * per_device, per_device, 0)  2.94 us

profile of v2, /device:TPU:0, one launch (start us, length us, event | category | flops | bytes accessed | tf_op | source)
XLA Modules:
  0.0 140.6 jit_solution(13266912328191409275)
XLA Ops:
  0.6 0.0 copy-start
  0.7 0.7 copy-done
  1.3 0.1 constant_dynamic-slice_fusion.2
  1.4 0.1 copy.19
  1.5 0.6 reshape.48.index_ref
  2.1 0.8 constant_dynamic-slice_fusion.1
  2.9 0.1 copy.20
  2.9 0.6 reshape.49.coef_ref
  3.6 0.7 broadcast_multiply_fusion
  4.3 0.7 add.49
  5.0 0.6 dynamic_slice.16.start_ref
  5.6 1.3 fusion.inverse_ref
  6.9 0.9 fusion.1
  7.7 0.1 copy.25
  7.8 0.1 rev.3
  7.9 0.1 pad.13
  8.0 0.1 copy.24
  8.1 0.1 pad_maximum_fusion.2
  8.2 0.7 pad_maximum_fusion.1.basis_ref
  8.9 11.0 %copy.27 = bf16[1,32,62,2048]{3,2,1,0:T(8,128)(2,1)} copy(bf16[1,32,62,2048]{3,1,2,0:T(8,128)(2,1)} %param.7) | data formatting | bytes 16252928 | tf_op args[0]
  19.9 0.0 copy-start.1
  19.9 0.0 copy-start.2
  19.9 0.0 copy-start.3
  19.9 56.4 %shard_map.86 = f32[2048,2048]{1,0:T(8,128)} custom-call(s32[96]{0:T(128)} %reshape.48.index_ref, f32[96]{0:T(128)} %reshape.49.coef_ref, s32[32]{0:T(128)} %dynamic_slice.16.start_ref, f32[32]{0:T(128)} %fusion.inverse_ref, bf16[32,62,2048]{2,1,0:T(8,128)(2,1)} %bitcast.22, f32[35,2,128]{2,1,0:T(2,128)} %pad_maximum_fusion.1.basis_ref), custom_call_target="tpu_custom_call" | custom-call | tf_op jit(solution)/shard_map/pallas_call | solution.py:135
  76.3 0.0 copy-done.1
  76.3 0.0 copy-done.2
  76.3 0.0 copy-done.3
  76.3 0.2 select_reduce_fusion
  76.5 0.1 reshape.51
  76.6 0.6 broadcast_in_dim.28.weight_ref
  77.2 59.9 %shard_map.87 = (f32[64,2048]{1,0:T(8,128)}, f32[8,128]{1,0:T(8,128)}) custom-call(f32[2,2,2,4,64,2048]{5,4,3,2,1,0:T(8,128)} %bitcast.21, f32[4,8,128]{2,1,0:T(8,128)} %broadcast_in_dim.28.weight_ref), custom_call_target="tpu_custom_call" | custom-call | tf_op jit(solution)/shard_map/pallas_call | solution.py:319
  137.2 1.2 broadcast_add_fusion.1
  138.4 1.1 broadcast_divide_fusion
  139.5 0.2 slice.22
  139.7 0.9 pad_maximum_fusion
  (7 shorter events, 0.1 us)
Async XLA Ops:
  0.6 0.7 copy-start
  19.9 56.4 %copy-start.1 = (s32[1,256]{1,0:T(1,128)S(1)}, s32[1,256]{1,0:T(1,128)}, u32[]{:S(2)}) copy-start(s32[1,256]{1,0:T(1,128)} %param.9) | copy-start | bytes 3076
  19.9 56.4 %copy-start.2 = (s32[1,256,1]{1,2,0:T(1,128)S(1)}, s32[1,256,1]{1,2,0:T(1,128)}, u32[]{:S(2)}) copy-start(s32[1,256,1]{1,2,0:T(1,128)} %param.8) | copy-start | bytes 3076
  19.9 56.4 %copy-start.3 = (f32[1,256]{1,0:T(1,128)S(1)}, f32[1,256]{1,0:T(1,128)}, u32[]{:S(2)}) copy-start(f32[1,256]{1,0:T(1,128)} %param.12) | copy-start | bytes 3076

commit v3 on v2

--- a/solution.py
+++ b/solution.py
@@ -45,15 +45,15 @@
     lax.fori_loop(0, n_basis, build, 0)
 
 
-def match_block(b, index_ref, coef_ref, blocks_ref, pixels, windows, down_table, across_table, n_terms):
+def match_block(b, params_ref, blocks_ref, pixels, windows, down_table, across_table, n_terms):
     in_rows, columns = blocks_ref.shape[1:]
     tiles = columns // LANES
     block = blocks_ref[b]
     pixels[0:in_rows, :] = block
     pixels[64 : 64 + in_rows, :] = block
-    picks = [index_ref[b * n_terms + t] for t in range(n_terms)]
+    picks = [params_ref[t, b].astype(jnp.int32) for t in range(n_terms)]
     rows = jnp.concatenate(
-        [coef_ref[b * n_terms + t] * down_table[picks[t]] for t in range(n_terms)], axis=0
+        [params_ref[n_terms + t, b] * down_table[picks[t]] for t in range(n_terms)], axis=0
     )
     rows_high = rows.astype(jnp.bfloat16).astype(jnp.float32)
     lane = lax.broadcasted_iota(jnp.int32, rows.shape, 1)
@@ -83,31 +83,34 @@
 
 def match_kernel(
     dense, n_terms, taps,
-    index_ref, coef_ref, start_ref, inverse_ref, blocks_ref, basis_ref, out_ref,
-    pixels, windows, down_table, across_table,
+    params_ref, blocks_hbm, basis_ref, out_ref,
+    blocks_ref, pixels, windows, down_table, across_table, load_sem,
 ):
     count = blocks_ref.shape[0]
+    load = pltpu.make_async_copy(blocks_hbm, blocks_ref, load_sem)
+    load.start()
     build_tables(basis_ref, down_table, across_table, basis_ref.shape[0], taps)
     pixels[...] = jnp.zeros_like(pixels)
     windows[...] = jnp.zeros_like(windows)
     if dense:
         out_ref[...] = jnp.zeros_like(out_ref)
+    load.wait()
 
     def body(step, carry):
         for k in range(2):
             b = step * 2 + k
             matched = match_block(
-                b, index_ref, coef_ref, blocks_ref, pixels.at[k], windows.at[k],
+                b, params_ref, blocks_ref, pixels.at[k], windows.at[k],
                 down_table, across_table, n_terms,
             )
             if dense:
-                start = start_ref[b]
+                start = params_ref[2 * n_terms, b].astype(jnp.int32)
                 first = jnp.minimum((start // 8) * 8, out_ref.shape[0] - 40)
                 row = lax.broadcasted_iota(jnp.int32, (40, 32), 0)
                 column = lax.broadcasted_iota(jnp.int32, (40, 32), 1)
                 place = (row - column == start - first).astype(jnp.float32).astype(jnp.bfloat16)
                 shifted = jnp.dot(place, matched, preferred_element_type=jnp.float32)
-                out_ref[pl.ds(pl.multiple_of(first, 8), 40), :] += inverse_ref[b] * shifted
+                out_ref[pl.ds(pl.multiple_of(first, 8), 40), :] += params_ref[2 * n_terms + 1, b] * shifted
             else:
                 out_ref[b] = matched
         return carry
@@ -115,10 +118,10 @@
     lax.fori_loop(0, count // 2, body, 0)
 
 
-def match_all(blocks, picks, coef, starts, inverse, psf_basis, n_patch, dense):
+def match_all(blocks, params, psf_basis, n_patch, dense):
     count, in_rows, columns = blocks.shape
     n_basis, _, taps = psf_basis.shape
-    n_terms = picks.shape[0] // count
+    n_terms = (params.shape[0] - 2) // 2
     half = (taps - 1) // 2
     tiles = columns // LANES
     down_line = jnp.pad(psf_basis[:, 0], ((0, 0), (0, 64 - taps)))
@@ -135,16 +138,18 @@
     return pl.pallas_call(
         functools.partial(match_kernel, dense, n_terms, taps),
         out_shape=out,
-        in_specs=[smem] * 4 + [vmem] * 2,
+        in_specs=[smem, pl.BlockSpec(memory_space=pl.ANY), vmem],
         out_specs=vmem,
         scratch_shapes=[
+            pltpu.VMEM(blocks.shape, jnp.bfloat16),
             pltpu.VMEM((2, 128, columns), jnp.bfloat16),
             pltpu.VMEM((2, (tiles + 1) * 64, n_terms * 2 * LANES), jnp.bfloat16),
             pltpu.VMEM((n_basis, 32, LANES), jnp.float32),
             pltpu.VMEM((n_basis, 2 * LANES, 2 * LANES), jnp.bfloat16),
+            pltpu.SemaphoreType.DMA,
         ],
         compiler_params=pltpu.CompilerParams(vmem_limit_bytes=VMEM_LIMIT),
-    )(picks, coef, starts, inverse, blocks, lines)
+    )(params, blocks, lines)
 
 
 def slots_route(matched, own_target, targets, row_offset, inverse, n_patch, own_patch):
@@ -187,10 +192,10 @@
 
 
 def route_kernel(
-    chunks, dense_ref, weight_ref, total_ref, weight_out_ref,
-    send_core, got_core, send_one, got_one, keep_one, send_two, got_two, keep_two,
+    chunks, dense_hbm, weight_ref, total_ref, weight_out_ref,
+    dense_ref, send_core, got_core, send_one, got_one, keep_one, send_two, got_two, keep_two,
     send_group, got_group, got_weight,
-    core_sems, one_sems, two_sems, group_sems, weight_sems,
+    core_sems, one_sems, two_sems, group_sems, weight_sems, load_sems,
 ):
     p, z = lax.axis_index("patch"), lax.axis_index("vgroup")
     n_group = dense_ref.shape[3]
@@ -203,6 +208,16 @@
     groups = [(z + d) % n_group for d in range(1, n_group)]
     across_z = [(p, to) for to in groups]
 
+    loads = []
+    for g in range(chunks):
+        cols = pl.ds(g * width, width)
+        loads.append(
+            pltpu.make_async_copy(
+                dense_hbm.at[:, :, :, :, :, cols], dense_ref.at[:, :, :, :, :, cols], load_sems.at[g]
+            )
+        )
+        loads[g].start()
+
     barrier = pltpu.get_barrier_semaphore()
     partners = [across_core, across_x, across_y] + across_z
     for partner in partners:
@@ -228,6 +243,7 @@
 
     def stage_core(g):
         cols = slice(g * width, (g + 1) * width)
+        loads[g].wait()
         send_core[g] = dense_ref[:, :, 1 - c, :, :, cols].astype(jnp.bfloat16)
         core_copies[g] = go(send_core.at[g], got_core.at[g], core_sems, (g,), across_core)
 
@@ -304,7 +320,7 @@
     columns = dense.shape[-1]
     share = PR // n_group
     half = n_group // 2
-    chunks = 4
+    chunks = 8
     width = columns // chunks
     peers = n_group - 1
     vmem = pl.BlockSpec(memory_space=pltpu.VMEM)
@@ -322,16 +338,17 @@
             jax.ShapeDtypeStruct((share, columns), jnp.float32),
             jax.ShapeDtypeStruct((8, LANES), jnp.float32),
         ),
-        in_specs=[vmem] * 2,
+        in_specs=[pl.BlockSpec(memory_space=pl.ANY), vmem],
         out_specs=(vmem, vmem),
         scratch_shapes=[
+            pltpu.VMEM(dense.shape, jnp.float32),
             buffer(2, 2, n_group), buffer(2, 2, n_group),
             buffer(2, 2, half), buffer(2, 2, half), buffer(2, 2, half, kind=jnp.float32),
             buffer(2, half), buffer(2, half), buffer(n_group, kind=jnp.float32),
             buffer(peers), buffer(peers),
             pltpu.VMEM((peers, 8, LANES), jnp.float32),
             sems((2, chunks)), sems((2, chunks, 2)), sems((2, chunks, 2)),
-            sems((2, chunks, peers)), sems((2, peers)),
+            sems((2, chunks, peers)), sems((2, peers)), sems((chunks,)),
         ],
         compiler_params=pltpu.CompilerParams(
             collective_id=0, has_side_effects=True, vmem_limit_bytes=VMEM_LIMIT
@@ -349,18 +366,23 @@
     out_rows = in_rows - taps + 1
     dense = n_patch == 8 and n_group % 2 == 0 and n_patch * PR * columns * 4 <= DENSE_LIMIT
 
-    def own(values):
-        return lax.dynamic_slice_in_dim(values, own_patch * per_device, per_device, 0)
-
     all_starts = target_patch[0, :, 0] * PR + row_offset[0]
-    starts, inverse = own(all_starts), own(inv_variance[0])
-    picks, coef = own(basis_index[0]).reshape(-1), own(basis_coef[0]).reshape(-1)
+    params = jnp.concatenate(
+        [
+            basis_index[0].T.astype(jnp.float32),
+            basis_coef[0].T,
+            all_starts.astype(jnp.float32)[None],
+            inv_variance,
+        ],
+        axis=0,
+    )
+    params = lax.dynamic_slice_in_dim(params, own_patch * per_device, per_device, 1)
 
     rows = (own_patch * PR + jnp.arange(PR, dtype=jnp.int32))[:, None]
     inside = jnp.logical_and(rows >= all_starts[None], rows < all_starts[None] + out_rows)
     weight = jnp.sum(jnp.where(inside, inv_variance[0][None], 0.0), axis=1)
 
-    result = match_all(blocks, picks, coef, starts, inverse, psf_basis, n_patch, dense)
+    result = match_all(blocks, params, psf_basis, n_patch, dense)
     if dense:
         numerator, weight = dense_route(result, weight, n_group)
     else:

time: 141 us -> 129 us (0.915)
  Pallas kernels: 116 us -> 107 us
  local copies, waits for them, and re-layouts: 18.1 us -> 13.9 us
    pallas_call x1, Pallas kernels: 59.9 us -> 53.6 us  [dense_route(): pl.pallas_call(functools.partial(route_kernel, chunks), out_shape=(jax.Sh...]
    dynamic_slice x6 -> x0, local copies, waits for them, and re-layouts: 2.94 us -> none  [own(): lax.dynamic_slice_in_dim(values, own_patch * per_device, per_device, 0)]
    pallas_call x1, Pallas kernels: 56.4 us -> 53.7 us  [match_all(): pl.pallas_call(functools.partial(match_kernel, dense, n_terms, taps), out...]
    unnamed x11 -> x6, local copies, waits for them, and re-layouts: 11.9 us -> 11.9 us
where the time goes in v3:
time: 129 us
  Pallas kernels  107 us (83%)
  local copies, waits for them, and re-layouts  13.9 us (11%)
  other arithmetic  6.86 us (5%)
    pallas_call x1, Pallas kernels, match_all(): pl.pallas_call(functools.partial(match_kernel, dense, n_terms, taps), out...  53.7 us
    pallas_call x1, Pallas kernels, dense_route(): pl.pallas_call(functools.partial(route_kernel, chunks), out_shape=(jax.Sh...  53.6 us
    unnamed x6, local copies, waits for them, and re-layouts  11.9 us

profile of v3, /device:TPU:0, one launch (start us, length us, event | category | flops | bytes accessed | tf_op | source)
XLA Modules:
  0.0 128.8 jit_solution(14484745066022701305)
XLA Ops:
  0.6 0.7 broadcast_add_fusion
  1.3 0.7 copy.26
  2.0 0.7 fusion.3
  2.7 1.3 %fusion.2.params_ref = f32[8,32]{1,0:T(8,128)} fusion(s32[]{:T(128)S(6)} %select_n.7, f32[3,256]{1,0:T(4,128)S(1)} %fusion.3, f32[3,256]{1,0:T(4,128)S(1)} %bitcast.30, f32[1,256]{1,0:T(1,128)S(1)} %convert_element_type.22, f32[1,256]{1,0:T(1,128)} %param.12), kind=kLoop, calls=%fused_computation.12 | loop fusion | flops 768 | bytes 9220 | tf_op jit(solution)/shard_map/concatenate | solution.py:370
  4.0 0.9 fusion.4
  4.9 0.1 copy.19
  5.0 0.1 rev.3
  5.1 0.1 pad.13
  5.2 0.1 copy.18
  5.3 0.1 pad_maximum_fusion.2
  5.4 0.7 pad_maximum_fusion.1.basis_ref
  6.0 11.0 %copy.25 = bf16[1,32,62,2048]{3,2,1,0:T(8,128)(2,1)} copy(bf16[1,32,62,2048]{3,1,2,0:T(8,128)(2,1)} %param.7) | data formatting | bytes 16252928 | tf_op args[0]
  17.1 0.0 copy-start
  17.1 53.7 %shard_map.86 = f32[2048,2048]{1,0:T(8,128)} custom-call(f32[8,32]{1,0:T(8,128)} %fusion.2.params_ref, bf16[32,62,2048]{2,1,0:T(8,128)(2,1)} %bitcast.27, f32[35,2,128]{2,1,0:T(2,128)} %pad_maximum_fusion.1.basis_ref), custom_call_target="tpu_custom_call" | custom-call | tf_op jit(solution)/shard_map/pallas_call | solution.py:138
  70.8 0.0 copy-done
  70.8 0.2 select_reduce_fusion
  71.0 0.1 reshape.38
  71.1 0.6 broadcast_in_dim.29.weight_ref
  71.7 53.6 %shard_map.87 = (f32[64,2048]{1,0:T(8,128)}, f32[8,128]{1,0:T(8,128)}) custom-call(f32[2,2,2,4,64,2048]{5,4,3,2,1,0:T(8,128)} %bitcast.26, f32[4,8,128]{2,1,0:T(8,128)} %broadcast_in_dim.29.weight_ref), custom_call_target="tpu_custom_call" | custom-call | tf_op jit(solution)/shard_map/pallas_call | solution.py:335
  125.3 1.2 broadcast_add_fusion.1
  126.5 1.1 broadcast_divide_fusion
  127.7 0.2 slice.22
  127.9 0.9 pad_maximum_fusion
  (7 shorter events, 0.1 us)
Async XLA Ops:
  17.1 53.7 %copy-start = (f32[1,256]{1,0:T(1,128)S(1)}, f32[1,256]{1,0:T(1,128)}, u32[]{:S(2)}) copy-start(f32[1,256]{1,0:T(1,128)} %param.12) | copy-start | bytes 3076
